TPU v7x, 512 devices: a whole 4x8x8 slice. The times are simulated.
512 devices in a mesh: row: 32 (over y, x_lo, core), col: 16 (over x_hi, z).
Axes of the slice: x: 4 (x_hi: 2, x_lo: 2; x = x_hi * 2 + x_lo), y: 8, z: 8, core: 2. Of those that a mesh axis runs over, the one named last changes fastest.
Arguments:
- object_slices: bfloat16 [2, 2, 4096, 2048], P(None, None, 'row', 'col'), may hold values from -4.1875 to 4.1875
- probe_modes: float32 [4, 2, 128, 128], replicated, may hold values from -3 to 3
- prop_phase: float32 [128, 128], replicated, may hold values from -3.140625 to 3.140625
- measured: float32 [2048, 128, 128], P(('row', 'col')), may hold values from 0 to 4
- counts: int32 [512], P(('row', 'col')), may hold values from 1 to 4, as said below
- coords: int32 [2048, 2], P(('row', 'col')), may hold values from 0 to 3968, as said below
Outputs:
- object_grad: float32 [2, 2, 4096, 2048], P(None, None, 'row', 'col')
- probe_grad: float32 [32, 4, 2, 128, 128], P('row')
Inputs may be any that keep to these rules, and one draw needn't show every extreme that they name: The first counts[d] of device d's 4 slots are live; some device holds 4 live slots in every draw. `coords`: rows d * 4 to (d + 1) * 4 - 1 belong to device d = i * (devices along col) + j: their pixel row lies in [i * 128, (i + 1) * 128), their pixel column in [j * 128, (j + 1) * 128), and every patch of 128 x 128 pixels lies inside the object.
All inputs are finite; a program needn't handle non-finite values.
Results may differ from a plain program's by a relative error of at most 0.024.
The roundings to bfloat16 on the way count: a program that leaves them out, or rounds other values in their place, can miss the bound.
Values may be sent and summed in bfloat16 or wider, within the bound.
No kernel may reach another device: no remote copies, remote signals or barrier semaphores. Data moves between devices by JAX's collectives and lax.ppermute only.
A program may use at most 64 MiB of HBM per device.

v0:
```python
import math

import jax
import jax.numpy as jnp
from jax import lax
from jax.sharding import PartitionSpec as P


def from_behind(block, axis, distance):
    devices = range(lax.axis_size(axis))
    route = [(i - distance, i) for i in devices if i - distance in devices]
    return lax.ppermute(block, axis, route)


def dft_tables(size):
    steps_idx = jnp.arange(size, dtype=jnp.int32)
    product_idx = steps_idx[:, None] * steps_idx[None, :] % size
    angle = product_idx.astype(jnp.float32) * (2.0 * math.pi / size)
    scale = 1.0 / math.sqrt(size)
    return (
        (jnp.cos(angle) * scale).astype(jnp.bfloat16),
        (jnp.sin(angle) * scale).astype(jnp.bfloat16),
    )


def transform(wave_real, wave_imag, orient, cos_table, sin_table):
    batch = wave_real.shape[0]
    size = wave_real.shape[-1]
    stacked = (
        jnp.concatenate([wave_real, wave_imag], 0)
        .astype(jnp.bfloat16)
        .reshape(2 * batch * size, size)
    )
    table = jnp.concatenate([cos_table, sin_table], 1)
    product = jnp.dot(stacked, table, preferred_element_type=jnp.float32).reshape(
        2, batch, size, 2, size
    )
    half_real = product[0, :, :, 0] - orient * product[1, :, :, 1]
    half_imag = orient * product[0, :, :, 1] + product[1, :, :, 0]
    halves = jnp.concatenate([half_real, half_imag], 0).astype(jnp.bfloat16)
    tables = jnp.stack([cos_table, sin_table])
    left = jnp.einsum("tjk,bkl->tbjl", tables, halves, preferred_element_type=jnp.float32)
    out_real = left[0, :batch] - orient * left[1, batch:]
    out_imag = orient * left[1, :batch] + left[0, batch:]
    return (out_real, out_imag)


def multiply(a_real, a_imag, b_real, b_imag):
    return (a_real * b_real - a_imag * b_imag, a_real * b_imag + a_imag * b_real)


def multiply_conj(a_real, a_imag, b_real, b_imag):
    return (a_real * b_real + a_imag * b_imag, a_imag * b_real - a_real * b_imag)


def position_grads(patch, probe_modes, prop_real, prop_imag, measured_one, cos_table, sin_table):
    layers = patch.shape[0]
    enter_real, enter_imag = (probe_modes[:, 0], probe_modes[:, 1])
    entering = []
    for which_layer in range(layers):
        entering.append((enter_real, enter_imag))
        leave_real, leave_imag = multiply(
            enter_real, enter_imag, patch[which_layer, 0], patch[which_layer, 1]
        )
        if which_layer < layers - 1:
            freq_real, freq_imag = transform(leave_real, leave_imag, -1.0, cos_table, sin_table)
            freq_real, freq_imag = multiply(freq_real, freq_imag, prop_real, prop_imag)
            enter_real, enter_imag = transform(freq_real, freq_imag, 1.0, cos_table, sin_table)
    far_real, far_imag = transform(leave_real, leave_imag, -1.0, cos_table, sin_table)
    residual = jnp.sum(far_real * far_real + far_imag * far_imag, 0) - measured_one
    back_real, back_imag = transform(
        residual * far_real, residual * far_imag, 1.0, cos_table, sin_table
    )
    slice_grads = [None] * layers
    for which_layer in reversed(range(layers)):
        ent_real, ent_imag = entering[which_layer]
        grad_real, grad_imag = multiply_conj(back_real, back_imag, ent_real, ent_imag)
        slice_grads[which_layer] = jnp.stack([jnp.sum(grad_real, 0), jnp.sum(grad_imag, 0)])
        to_real, to_imag = multiply_conj(
            back_real, back_imag, patch[which_layer, 0], patch[which_layer, 1]
        )
        if which_layer > 0:
            freq_real, freq_imag = transform(to_real, to_imag, -1.0, cos_table, sin_table)
            freq_real, freq_imag = multiply_conj(freq_real, freq_imag, prop_real, prop_imag)
            back_real, back_imag = transform(freq_real, freq_imag, 1.0, cos_table, sin_table)
    return (jnp.stack(slice_grads), jnp.stack([to_real, to_imag], 1))


def body(object_slices, probe_modes, prop_phase, measured, counts, coords):
    size = probe_modes.shape[-1]
    layers = object_slices.shape[0]
    tile_rows = object_slices.shape[2]
    tile_cols = object_slices.shape[3]
    col_count = lax.axis_size("col")
    row_index = lax.axis_index("row")
    col_index = lax.axis_index("col")
    lower = from_behind(object_slices, "row", -1)
    taller = jnp.concatenate([object_slices, lower], 2)
    side = from_behind(taller, "col", -1)
    extended = jnp.concatenate([taller, side], 3)
    cos_table, sin_table = dft_tables(size)
    prop_real = jnp.cos(prop_phase)
    prop_imag = jnp.sin(prop_phase)
    zero_idx = jnp.zeros((), jnp.int32)
    start_row = row_index * tile_rows
    start_col = col_index * tile_cols

    def visit(slot, carry):
        ext_grad, probe_acc = carry
        local_row = coords[slot, 0] - start_row
        local_col = coords[slot, 1] - start_col
        starts = (zero_idx, zero_idx, local_row, local_col)
        patch = lax.dynamic_slice(extended, starts, (layers, 2, size, size)).astype(jnp.float32)
        grads, probe_part = position_grads(
            patch, probe_modes, prop_real, prop_imag, measured[slot], cos_table, sin_table
        )
        current = lax.dynamic_slice(ext_grad, starts, (layers, 2, size, size))
        ext_grad = lax.dynamic_update_slice(ext_grad, current + grads, starts)
        return (ext_grad, probe_acc + probe_part)

    init = (jnp.zeros(extended.shape, jnp.float32), jnp.zeros(probe_modes.shape, jnp.float32))
    ext_grad, probe_acc = lax.fori_loop(0, counts[0], visit, init)
    side_back = from_behind(ext_grad[:, :, :, tile_cols:].astype(jnp.bfloat16), "col", 1).astype(
        jnp.float32
    )
    ext_grad = ext_grad.at[:, :, :, :size].add(side_back)
    lower_back = from_behind(
        ext_grad[:, :, tile_rows:, :tile_cols].astype(jnp.bfloat16), "row", 1
    ).astype(jnp.float32)
    owned = ext_grad[:, :, :tile_rows, :tile_cols].at[:, :, :size, :].add(lower_back)
    region_slots = measured.shape[0] * col_count
    probe_total = lax.psum(probe_acc.astype(jnp.bfloat16), "col").astype(jnp.float32)
    return (owned, (probe_total * (1.0 / math.sqrt(region_slots)))[None])


def solution(mesh):
    return jax.shard_map(
        body,
        mesh=mesh,
        in_specs=(
            P(None, None, "row", "col"),
            P(),
            P(),
            P(("row", "col"), None, None),
            P(("row", "col")),
            P(("row", "col"), None),
        ),
        out_specs=(P(None, None, "row", "col"), P("row", None, None, None, None)),
        check_vma=False,
    )
```

profile of v0, /device:TPU:56, one launch (start us, length us, event | category | flops | bytes accessed | tf_op | source)
XLA Modules:
  0.0 269.3 jit_solution(13700938638897728298)
XLA Ops:
  7.2 1.0 copy.98
  8.3 3.8 %collective-permute-start = (bf16[2,2,128,128]{2,3,1,0:T(8,128)(2,1)S(1)}, bf16[2,2,128,128]{2,3,1,0:T(8,128)(2,1)S(1)}, u32[]{:S(2)}, u32[]{:S(2)}) collective-permute-start(bf16[2,2,128,128]{2,3,1,0:T(8,128)(2,1)S(1)} %copy.98), channel_id=1, source_target_pairs={{16,0},{32,16},{48,32},{64,48},{80,64},{96,80},{112,96},{128,112},... | collective-permute-start | bytes 393224 | tf_op jit(solution)/shard_map/ppermute | solution.py:12
  12.0 0.3 multiply_convert_fusion.4
  12.3 0.3 multiply_convert_fusion.2
  12.6 1.9 collective-permute-done
  14.5 1.3 collective-permute-start.1
  15.9 0.8 copy-done.4
  16.7 0.1 copy.99
  16.8 0.2 copy.101
  17.0 0.2 fusion.103
  17.3 8.1 %collective-permute-done.1 = bf16[2,2,256,128]{2,3,1,0:T(8,128)(2,1)S(1)} collective-permute-done((bf16[2,2,256,128]{2,3,1,0:T(8,128)(2,1)S(1)}, bf16[2,2,256,128]{2,3,1,0:T(8,128)(2,1)S(1)}, u32[]{:S(2)}, u32[]{:S(2)}) %collective-permute-start.1) | collective-permute-done | bytes 262176 | tf_op jit(solution)/shard_map/ppermute | solution.py:12
  25.4 1.1 broadcast_in_dim.6.clone
  26.5 0.6 copy-done.5
  27.1 16.1 %while.17 = (s32[]{:T(128)}, f32[2,2,256,256]{3,2,1,0:T(8,128)}, f32[4,2,128,128]{2,3,0,1:T(8,128)S(1)}, s32[]{:T(128)}, s32[4,2]{0,1:T(2,128)S(1)}, /*index=5*/...) while((s32[]{:T(128)}, f32[2,2,256,256]{3,2,1,0:T(8,128)}, ...), condition=%wide.region_6.7_spmd, body=%wide.region_0.6_spmd.sunk | while | flops 817692672 | bytes 54329732 | solution.py:122
  27.8 0.7 constant_dynamic-slice_fusion.7
  29.8 0.1 dynamic-slice_convert_fusion.2
  29.9 0.1 fusion.179
  30.1 0.3 fusion.180
  30.5 0.3 convolution_bitcast_fusion.12
  30.8 0.1 subtract_convert_fusion.6
  31.0 0.3 fusion.183
  31.4 0.3 convolution_bitcast_fusion.13
  31.9 0.3 fusion.186
  32.3 0.3 convolution_bitcast_fusion.14
  32.7 0.9 constant_dynamic-slice_fusion.9
  33.5 0.1 copy.169
  33.6 0.1 multiply_convert_fusion.7
  33.8 0.3 fusion.189
  34.2 0.3 convolution_bitcast_fusion.15
  34.6 0.1 add_reduce_fusion.5
  34.7 0.3 fusion.192
  35.1 0.3 convolution_bitcast_fusion.16
  35.5 0.1 add_convert_fusion.9
  35.6 0.3 fusion.194
  36.0 0.3 convolution_bitcast_fusion.17
  36.5 0.1 maximum_add_fusion.5
  36.7 1.2 constant_dynamic-slice_fusion.8
  37.9 0.1 copy.168
  38.1 0.1 copy.170
  38.2 4.3 %dynamic_update_slice.6 = f32[2,2,256,256]{3,2,1,0:T(8,128)} dynamic-update-slice(f32[2,2,256,256]{3,2,1,0:T(8,128)} %get-tuple-element.471, f32[2,2,128,128]{3,2,1,0:T(8,128)S(1)} %copy.170, s32[]{:T(128)} %constant.110.clone.1..sunk, s32[]{:T(128)} %constant.110.clone.1..sunk, s32[]{:T(128)S(6)} %select_n.66, s32[]{:T(128)S(6)} %select_n.67) | dynamic-update-slice | bytes 524292 | tf_op jit(solution)/shard_map/while/body/dynamic_update_slice | solution.py:118
  43.2 1.2 slice.663
  44.4 4.1 %collective-permute-start.2 = (bf16[2,2,256,128]{3,2,1,0:T(8,128)(2,1)S(1)}, bf16[2,2,256,128]{3,2,1,0:T(8,128)(2,1)S(1)}, u32[]{:S(2)}, u32[]{:S(2)}) collective-permute-start(bf16[2,2,256,128]{3,2,1,0:T(8,128)(2,1)S(1)} %slice.663), channel_id=1, source_target_pairs={{0,1},{1,2},{2,3},{3,4},{4,5},{5,6},{6,7},{7,8},{8,9},{9,10},{10,1... | collective-permute-start | bytes 786440 | tf_op jit(solution)/shard_map/ppermute | solution.py:12
  48.5 0.8 copy.105
  49.4 3.0 %collective-permute-done.2 = bf16[2,2,256,128]{3,2,1,0:T(8,128)(2,1)S(1)} collective-permute-done((bf16[2,2,256,128]{3,2,1,0:T(8,128)(2,1)S(1)}, bf16[2,2,256,128]{3,2,1,0:T(8,128)(2,1)S(1)}, u32[]{:S(2)}, u32[]{:S(2)}) %collective-permute-start.2) | collective-permute-done | bytes 262176 | tf_op jit(solution)/shard_map/ppermute | solution.py:12
  52.4 16.3 %collective-permute-start.3 = (bf16[2,2,128,128]{3,2,1,0:T(8,128)(2,1)S(1)}, bf16[2,2,128,128]{3,2,1,0:T(8,128)(2,1)S(1)}, u32[]{:S(2)}, u32[]{:S(2)}) collective-permute-start(bf16[2,2,128,128]{3,2,1,0:T(8,128)(2,1)S(1)} %slice.664), channel_id=1, source_target_pairs={{0,16},{16,32},{32,48},{48,64},{64,80},{80,96},{96,112},{112,128},... | collective-permute-start | bytes 393224 | tf_op jit(solution)/shard_map/ppermute | solution.py:12
  68.8 191.1 %all-reduce.2.cloned.1.call-done = bf16[4,2,128,128]{3,2,1,0:T(8,128)(2,1)} async-done(((bf16[4,2,128,128]{3,2,1,0:T(8,128)(2,1)}), bf16[4,2,128,128]{3,2,1,0:T(8,128)(2,1)}) %all-reduce.2.cloned.1.call-update) | async-done | bytes 262160 | tf_op jit(solution)/shard_map/psum | solution.py:132
  259.9 1.8 multiply_bitcast_fusion
  261.7 0.7 slice_add_fusion.12
  (47 shorter events, 1.4 us)
Async XLA Ops:
  7.2 252.7 %all-reduce.2.cloned.1.call-start = ((), (), s32[]{:S(2)}) async-start(), calls=%async_computation | async-start | bytes 524288 | tf_op jit(solution)/shard_map/psum | solution.py:132
  8.2 8.6 %copy-start.3 = (f32[4,2,128,128]{3,2,1,0:T(8,128)S(1)}, f32[4,2,128,128]{3,2,1,0:T(8,128)}, u32[]{:S(2)}) copy-start(f32[4,2,128,128]{3,2,1,0:T(8,128)} %param.15) | copy-start | bytes 1572868
  8.3 6.3 %collective-permute-start = (bf16[2,2,128,128]{2,3,1,0:T(8,128)(2,1)S(1)}, bf16[2,2,128,128]{2,3,1,0:T(8,128)(2,1)S(1)}, u32[]{:S(2)}, u32[]{:S(2)}) collective-permute-start(bf16[2,2,128,128]{2,3,1,0:T(8,128)(2,1)S(1)} %copy.98), channel_id=1, source_target_pairs={{16,0},{32,16},{48,32},{64,48},{80,64},{96,80},{112,96},{128,112},... | collective-permute-start | bytes 393224 | tf_op jit(solution)/shard_map/ppermute | solution.py:12
  14.5 10.8 %collective-permute-start.1 = (bf16[2,2,256,128]{2,3,1,0:T(8,128)(2,1)S(1)}, bf16[2,2,256,128]{2,3,1,0:T(8,128)(2,1)S(1)}, u32[]{:S(2)}, u32[]{:S(2)}) collective-permute-start(bf16[2,2,256,128]{2,3,1,0:T(8,128)(2,1)S(1)} %pad_maximum_fusion.7), channel_id=1, source_target_pairs={{1,0},{2,1},{3,2},{4,3},{5,4},{6,5},{7,6},{8,7},{9,8},{10,9},{11,1... | collective-permute-start | bytes 786440 | tf_op jit(solution)/shard_map/ppermute | solution.py:12
  15.8 0.8 copy-start.4
  26.4 0.7 copy-start.5
  27.8 2.2 copy-start.1
  38.2 4.3 %copy-start.2 = (bf16[2,2,256,256]{2,3,1,0:T(8,128)(2,1)S(1)}, bf16[2,2,256,256]{2,3,1,0:T(8,128)(2,1)}, u32[]{:S(2)}) copy-start(bf16[2,2,256,256]{2,3,1,0:T(8,128)(2,1)} %copy-done.1) | copy-start | bytes 1572868 | tf_op jit(solution)/shard_map/while
  43.2 9.2 %copy-start = (f32[2,2,256,256]{3,2,1,0:T(8,128)S(1)}, f32[2,2,256,256]{3,2,1,0:T(8,128)}, u32[]{:S(2)}) copy-start(f32[2,2,256,256]{3,2,1,0:T(8,128)} %get-tuple-element.200) | copy-start | bytes 3145732
  44.4 8.0 %collective-permute-start.2 = (bf16[2,2,256,128]{3,2,1,0:T(8,128)(2,1)S(1)}, bf16[2,2,256,128]{3,2,1,0:T(8,128)(2,1)S(1)}, u32[]{:S(2)}, u32[]{:S(2)}) collective-permute-start(bf16[2,2,256,128]{3,2,1,0:T(8,128)(2,1)S(1)} %slice.663), channel_id=1, source_target_pairs={{0,1},{1,2},{2,3},{3,4},{4,5},{5,6},{6,7},{7,8},{8,9},{9,10},{10,1... | collective-permute-start | bytes 786440 | tf_op jit(solution)/shard_map/ppermute | solution.py:12
  52.4 209.2 %collective-permute-start.3 = (bf16[2,2,128,128]{3,2,1,0:T(8,128)(2,1)S(1)}, bf16[2,2,128,128]{3,2,1,0:T(8,128)(2,1)S(1)}, u32[]{:S(2)}, u32[]{:S(2)}) collective-permute-start(bf16[2,2,128,128]{3,2,1,0:T(8,128)(2,1)S(1)} %slice.664), channel_id=1, source_target_pairs={{0,16},{16,32},{32,48},{48,64},{64,80},{80,96},{96,112},{112,128},... | collective-permute-start | bytes 393224 | tf_op jit(solution)/shard_map/ppermute | solution.py:12
Sparse Core Ops, SparseCore 0:
  49.5 210.3 all-reduce.1
where the time goes:
time: 271 us; the launch traced here: 269 us
  waiting for transfers between devices  204 us (75%)
  starting transfers between devices  25.5 us (9%)
  between operations  14.2 us (5%)
  local copies, waits for them, and re-layouts  13.6 us (5%)
  other arithmetic  5.03 us (2%)
  matrix products  3.9 us (1%)
  loops' own time  2.93 us (1%)
    psum x1, waiting for transfers between devices, body(): lax.psum(probe_acc.astype(jnp.bfloat16), 'col').astype(jnp.float32)  191 us
    ppermute x4, starting transfers between devices, from_behind(): return lax.ppermute(block, axis, route)  25.5 us
    ppermute x4, waiting for transfers between devices, from_behind(): return lax.ppermute(block, axis, route)  13 us
  transfers between devices with their start and end apart: 5, of which 4 were waited for; matrix products, arithmetic and copies ran while one was open for 1% of the time, Pallas kernels for 0%

commit v1 on v0

--- a/solution.py
+++ b/solution.py
@@ -129,7 +129,13 @@
     ).astype(jnp.float32)
     owned = ext_grad[:, :, :tile_rows, :tile_cols].at[:, :, :size, :].add(lower_back)
     region_slots = measured.shape[0] * col_count
-    probe_total = lax.psum(probe_acc.astype(jnp.bfloat16), "col").astype(jnp.float32)
+    shares = probe_acc.astype(jnp.bfloat16).reshape(col_count, -1, probe_acc.shape[-1])
+    received = lax.all_to_all(shares, "col", 0, 0, tiled=True)
+    share = jnp.sum(received.astype(jnp.float32), 0).astype(jnp.bfloat16)
+    spread = lax.all_to_all(
+        jnp.broadcast_to(share[None], shares.shape), "col", 0, 0, tiled=True
+    )
+    probe_total = spread.reshape(probe_acc.shape).astype(jnp.float32)
     return (owned, (probe_total * (1.0 / math.sqrt(region_slots)))[None])
 
 

time: 271 us -> 133 us (0.49)
  the two profiles are of different devices: /device:TPU:56 before, /device:TPU:16 now
where the time goes in v1:
time: 133 us; the launch traced here: 131 us
  starting transfers between devices  77.1 us (58%)
  waiting for transfers between devices  27.2 us (20%)
  local copies, waits for them, and re-layouts  13 us (10%)
  other arithmetic  5.9 us (4%)
  matrix products  3.93 us (3%)
  loops' own time  2.97 us (2%)
    all_to_all x1, starting transfers between devices, body(): received = lax.all_to_all(shares, 'col', 0, 0, tiled=True)  61 us
    ppermute x4, waiting for transfers between devices, from_behind(): return lax.ppermute(block, axis, route)  15.3 us
    ppermute x4, starting transfers between devices, from_behind(): return lax.ppermute(block, axis, route)  10.2 us
    all_to_all x1, waiting for transfers between devices, body(): received = lax.all_to_all(shares, 'col', 0, 0, tiled=True)  7.56 us
    all_to_all x1, starting transfers between devices, body(): lax.all_to_all(jnp.broadcast_to(share[None], shares.shape), 'col', 0, 0,...  5.83 us
    dynamic_update_slice x2, local copies, waits for them, and re-layouts, visit(): ext_grad = lax.dynamic_update_slice(ext_grad, current + grads, starts)  4.29 us
    all_to_all x1, waiting for transfers between devices, body(): lax.all_to_all(jnp.broadcast_to(share[None], shares.shape), 'col', 0, 0,...  4.29 us
    another operation x1, loops' own time, body(): ext_grad, probe_acc = lax.fori_loop(0, counts[0], visit, init)  2.97 us
  transfers between devices with their start and end apart: 6, of which 5 were waited for; matrix products, arithmetic and copies ran while one was open for 2% of the time, Pallas kernels for 0%

profile of v1, /device:TPU:16, one launch (start us, length us, event | category | flops | bytes accessed | tf_op | source)
XLA Modules:
  0.0 130.9 jit_solution(11611762101940936917)
XLA Ops:
  0.6 1.0 copy.145
  1.7 2.9 %collective-permute-start = (bf16[2,2,128,128]{2,3,1,0:T(8,128)(2,1)S(1)}, bf16[2,2,128,128]{2,3,1,0:T(8,128)(2,1)S(1)}, u32[]{:S(2)}, u32[]{:S(2)}) collective-permute-start(bf16[2,2,128,128]{2,3,1,0:T(8,128)(2,1)S(1)} %copy.145), channel_id=1, source_target_pairs={{16,0},{32,16},{48,32},{64,48},{80,64},{96,80},{112,96},{128,112},... | collective-permute-start | bytes 393224 | tf_op jit(solution)/shard_map/ppermute | solution.py:12
  4.5 0.3 multiply_convert_fusion.4
  4.8 0.3 multiply_convert_fusion.2
  5.1 1.9 %collective-permute-done = bf16[2,2,128,128]{2,3,1,0:T(8,128)(2,1)S(1)} collective-permute-done((bf16[2,2,128,128]{2,3,1,0:T(8,128)(2,1)S(1)}, bf16[2,2,128,128]{2,3,1,0:T(8,128)(2,1)S(1)}, u32[]{:S(2)}, u32[]{:S(2)}) %collective-permute-start) | collective-permute-done | bytes 131104 | tf_op jit(solution)/shard_map/ppermute | solution.py:12
  7.1 1.3 collective-permute-start.1
  8.4 0.8 copy-done.2
  9.3 0.2 copy.148
  9.5 0.2 fusion.103
  9.8 8.5 %collective-permute-done.1 = bf16[2,2,256,128]{2,3,1,0:T(8,128)(2,1)S(1)} collective-permute-done((bf16[2,2,256,128]{2,3,1,0:T(8,128)(2,1)S(1)}, bf16[2,2,256,128]{2,3,1,0:T(8,128)(2,1)S(1)}, u32[]{:S(2)}, u32[]{:S(2)}) %collective-permute-start.1) | collective-permute-done | bytes 262176 | tf_op jit(solution)/shard_map/ppermute | solution.py:12
  18.3 0.8 pad_maximum_fusion.6
  19.1 1.1 broadcast_in_dim.6.clone
  20.2 0.6 copy-done.3
  20.8 16.9 %while.17 = (s32[]{:T(128)}, f32[2,2,256,256]{3,2,1,0:T(8,128)}, f32[4,2,128,128]{2,3,0,1:T(8,128)S(1)}, s32[]{:T(128)}, s32[4,2]{0,1:T(2,128)S(1)}, /*index=5*/...) while((s32[]{:T(128)}, f32[2,2,256,256]{3,2,1,0:T(8,128)}, ...), condition=%wide.region_6.7_spmd, body=%wide.region_0.6_spmd.sunk | while | flops 817692672 | bytes 50135372 | solution.py:122
  21.5 0.7 constant_dynamic-slice_fusion.7
  23.5 1.1 dynamic-slice_convert_fusion.2
  24.8 0.3 fusion.180
  25.2 0.3 convolution_bitcast_fusion.12
  25.5 0.1 subtract_convert_fusion.6
  25.7 0.3 fusion.183
  26.1 0.3 convolution_bitcast_fusion.13
  26.6 0.3 fusion.186
  27.0 0.3 convolution_bitcast_fusion.14
  27.4 0.9 constant_dynamic-slice_fusion.9
  28.5 0.3 fusion.189
  28.9 0.3 convolution_bitcast_fusion.15
  29.3 0.1 add_reduce_fusion.5
  29.4 0.3 fusion.192
  29.8 0.3 convolution_bitcast_fusion.16
  30.2 0.1 add_convert_fusion.9
  30.3 0.3 fusion.194
  30.7 0.3 convolution_bitcast_fusion.17
  31.2 0.1 maximum_add_fusion.5
  31.4 1.2 constant_dynamic-slice_fusion.8
  32.6 0.1 copy.215
  32.8 0.1 copy.217
  33.0 4.2 %dynamic_update_slice.6 = f32[2,2,256,256]{3,2,1,0:T(8,128)} dynamic-update-slice(f32[2,2,256,256]{3,2,1,0:T(8,128)} %get-tuple-element.485, f32[2,2,128,128]{3,2,1,0:T(8,128)S(1)} %copy.217, s32[]{:T(128)} %constant.112.clone.1..sunk, s32[]{:T(128)} %constant.112.clone.1..sunk, s32[]{:T(128)S(6)} %select_n.66, s32[]{:T(128)S(6)} %select_n.67) | dynamic-update-slice | bytes 524292 | tf_op jit(solution)/shard_map/while/body/dynamic_update_slice | solution.py:118
  37.8 0.8 copy.152
  38.6 61.0 %all-to-all-start = ((bf16[16,64,128]{2,1,0:T(8,128)(2,1)}), bf16[16,64,128]{2,1,0:T(8,128)(2,1)S(1)}, u32[]{:S(2)}, u32[]{:S(2)}) async-start(bf16[16,64,128]{2,1,0:T(8,128)(2,1)} %bitcast.79), calls=%async_computation | async-start | bytes 524288 | tf_op jit(solution)/shard_map/all_to_all | solution.py:133
  99.7 3.8 %collective-permute-start.2 = (bf16[2,2,256,128]{3,2,1,0:T(8,128)(2,1)S(1)}, bf16[2,2,256,128]{3,2,1,0:T(8,128)(2,1)S(1)}, u32[]{:S(2)}, u32[]{:S(2)}) collective-permute-start(bf16[2,2,256,128]{3,2,1,0:T(8,128)(2,1)S(1)} %slice.663), channel_id=1, source_target_pairs={{0,1},{1,2},{2,3},{3,4},{4,5},{5,6},{6,7},{7,8},{8,9},{9,10},{10,1... | collective-permute-start | bytes 786440 | tf_op jit(solution)/shard_map/ppermute | solution.py:12
  103.6 7.6 %all-to-all-done = bf16[16,64,128]{2,1,0:T(8,128)(2,1)S(1)} async-done(((bf16[16,64,128]{2,1,0:T(8,128)(2,1)}), bf16[16,64,128]{2,1,0:T(8,128)(2,1)S(1)}, u32[]{:S(2)}, u32[]{:S(2)}) %all-to-all-start) | async-done | bytes 262176 | tf_op jit(solution)/shard_map/all_to_all | solution.py:133
  111.2 0.8 broadcast_in_dim.8
  111.9 5.8 %all-to-all-start.1 = ((bf16[16,64,128]{2,1,0:T(8,128)(2,1)}), bf16[16,64,128]{2,1,0:T(8,128)(2,1)S(1)}, u32[]{:S(2)}, u32[]{:S(2)}) async-start(bf16[16,64,128]{2,1,0:T(8,128)(2,1)} %broadcast_in_dim.8), calls=%async_computation.1 | async-start | bytes 524288 | tf_op jit(solution)/shard_map/all_to_all | solution.py:135
  117.9 2.3 %collective-permute-start.3 = (bf16[2,2,128,128]{3,2,1,0:T(8,128)(2,1)S(1)}, bf16[2,2,128,128]{3,2,1,0:T(8,128)(2,1)S(1)}, u32[]{:S(2)}, u32[]{:S(2)}) collective-permute-start(bf16[2,2,128,128]{3,2,1,0:T(8,128)(2,1)S(1)} %slice.664), channel_id=1, source_target_pairs={{0,16},{16,32},{32,48},{48,64},{64,80},{80,96},{96,112},{112,128},... | collective-permute-start | bytes 393224 | tf_op jit(solution)/shard_map/ppermute | solution.py:12
  120.1 4.9 %collective-permute-done.3 = bf16[2,2,128,128]{3,2,1,0:T(8,128)(2,1)S(1)} collective-permute-done((bf16[2,2,128,128]{3,2,1,0:T(8,128)(2,1)S(1)}, bf16[2,2,128,128]{3,2,1,0:T(8,128)(2,1)S(1)}, u32[]{:S(2)}, u32[]{:S(2)}) %collective-permute-start.3) | collective-permute-done | bytes 131104 | tf_op jit(solution)/shard_map/ppermute | solution.py:12
  125.0 0.7 slice_add_fusion.12
  125.8 4.3 %all-to-all-done.1 = bf16[16,64,128]{2,1,0:T(8,128)(2,1)S(1)} async-done(((bf16[16,64,128]{2,1,0:T(8,128)(2,1)}), bf16[16,64,128]{2,1,0:T(8,128)(2,1)S(1)}, u32[]{:S(2)}, u32[]{:S(2)}) %all-to-all-start.1) | async-done | bytes 262176 | tf_op jit(solution)/shard_map/all_to_all | solution.py:135
  130.1 0.8 convert_multiply_fusion
  (46 shorter events, 1.6 us)
Async XLA Ops:
  1.7 7.7 %copy-start.1 = (f32[4,2,128,128]{3,2,1,0:T(8,128)S(1)}, f32[4,2,128,128]{3,2,1,0:T(8,128)}, u32[]{:S(2)}) copy-start(f32[4,2,128,128]{3,2,1,0:T(8,128)} %param.15) | copy-start | bytes 1572868
  1.7 5.4 %collective-permute-start = (bf16[2,2,128,128]{2,3,1,0:T(8,128)(2,1)S(1)}, bf16[2,2,128,128]{2,3,1,0:T(8,128)(2,1)S(1)}, u32[]{:S(2)}, u32[]{:S(2)}) collective-permute-start(bf16[2,2,128,128]{2,3,1,0:T(8,128)(2,1)S(1)} %copy.145), channel_id=1, source_target_pairs={{16,0},{32,16},{48,32},{64,48},{80,64},{96,80},{112,96},{128,112},... | collective-permute-start | bytes 393224 | tf_op jit(solution)/shard_map/ppermute | solution.py:12
  7.1 11.2 %collective-permute-start.1 = (bf16[2,2,256,128]{2,3,1,0:T(8,128)(2,1)S(1)}, bf16[2,2,256,128]{2,3,1,0:T(8,128)(2,1)S(1)}, u32[]{:S(2)}, u32[]{:S(2)}) collective-permute-start(bf16[2,2,256,128]{2,3,1,0:T(8,128)(2,1)S(1)} %pad_maximum_fusion.7), channel_id=1, source_target_pairs={{1,0},{2,1},{3,2},{4,3},{5,4},{6,5},{7,6},{8,7},{9,8},{10,9},{11,1... | collective-permute-start | bytes 786440 | tf_op jit(solution)/shard_map/ppermute | solution.py:12
  8.4 0.8 copy-start.2
  20.2 0.7 copy-start.3
  37.8 61.9 %copy-start = (f32[2,2,256,256]{3,2,1,0:T(8,128)S(1)}, f32[2,2,256,256]{3,2,1,0:T(8,128)}, u32[]{:S(2)}) copy-start(f32[2,2,256,256]{3,2,1,0:T(8,128)} %get-tuple-element.200) | copy-start | bytes 3145732
  38.6 72.5 %all-to-all-start = ((bf16[16,64,128]{2,1,0:T(8,128)(2,1)}), bf16[16,64,128]{2,1,0:T(8,128)(2,1)S(1)}, u32[]{:S(2)}, u32[]{:S(2)}) async-start(bf16[16,64,128]{2,1,0:T(8,128)(2,1)} %bitcast.79), calls=%async_computation | async-start | bytes 524288 | tf_op jit(solution)/shard_map/all_to_all | solution.py:133
  99.7 18.1 %collective-permute-start.2 = (bf16[2,2,256,128]{3,2,1,0:T(8,128)(2,1)S(1)}, bf16[2,2,256,128]{3,2,1,0:T(8,128)(2,1)S(1)}, u32[]{:S(2)}, u32[]{:S(2)}) collective-permute-start(bf16[2,2,256,128]{3,2,1,0:T(8,128)(2,1)S(1)} %slice.663), channel_id=1, source_target_pairs={{0,1},{1,2},{2,3},{3,4},{4,5},{5,6},{6,7},{7,8},{8,9},{9,10},{10,1... | collective-permute-start | bytes 786440 | tf_op jit(solution)/shard_map/ppermute | solution.py:12
  111.9 18.1 %all-to-all-start.1 = ((bf16[16,64,128]{2,1,0:T(8,128)(2,1)}), bf16[16,64,128]{2,1,0:T(8,128)(2,1)S(1)}, u32[]{:S(2)}, u32[]{:S(2)}) async-start(bf16[16,64,128]{2,1,0:T(8,128)(2,1)} %broadcast_in_dim.8), calls=%async_computation.1 | async-start | bytes 524288 | tf_op jit(solution)/shard_map/all_to_all | solution.py:135
  117.9 7.2 %collective-permute-start.3 = (bf16[2,2,128,128]{3,2,1,0:T(8,128)(2,1)S(1)}, bf16[2,2,128,128]{3,2,1,0:T(8,128)(2,1)S(1)}, u32[]{:S(2)}, u32[]{:S(2)}) collective-permute-start(bf16[2,2,128,128]{3,2,1,0:T(8,128)(2,1)S(1)} %slice.664), channel_id=1, source_target_pairs={{0,16},{16,32},{32,48},{48,64},{64,80},{80,96},{96,112},{112,128},... | collective-permute-start | bytes 393224 | tf_op jit(solution)/shard_map/ppermute | solution.py:12

commit v2 on v1

v2 whole, which is shorter than its diff:
```python
import functools
import math

import jax
import jax.numpy as jnp
from jax import lax
from jax.experimental import pallas as pl
from jax.experimental.pallas import tpu as pltpu
from jax.sharding import PartitionSpec as P

GROUP = 2


def from_behind(block, axis, distance):
    devices = range(lax.axis_size(axis))
    route = [(i - distance, i) for i in devices if i - distance in devices]
    return lax.ppermute(block, axis, route)


def dft_matrices(size):
    steps_idx = jnp.arange(size, dtype=jnp.int32)
    product_idx = steps_idx[:, None] * steps_idx[None, :] % size
    angle = product_idx.astype(jnp.float32) * (2.0 * math.pi / size)
    scale = 1.0 / math.sqrt(size)
    cos_table = (jnp.cos(angle) * scale).astype(jnp.bfloat16)
    sin_table = (jnp.sin(angle) * scale).astype(jnp.bfloat16)
    minus = jnp.concatenate(
        [
            jnp.concatenate([cos_table, -sin_table], 1),
            jnp.concatenate([sin_table, cos_table], 1),
        ],
        0,
    )
    plus = jnp.concatenate(
        [
            jnp.concatenate([cos_table, sin_table], 1),
            jnp.concatenate([-sin_table, cos_table], 1),
        ],
        0,
    )
    return jnp.stack([minus, plus])


def swap_blocks(matrix, size):
    upper = jnp.concatenate([matrix[:size, :size], matrix[size:, :size]], 1)
    lower = jnp.concatenate([matrix[:size, size:], matrix[size:, size:]], 1)
    return jnp.concatenate([upper, lower], 0)


def transform(real, imag, first, second):
    size = real.shape[0]
    stacked = jnp.concatenate([real, imag], 0).astype(jnp.bfloat16)
    half = jnp.dot(
        swap_blocks(stacked, size), first, preferred_element_type=jnp.float32
    ).astype(jnp.bfloat16)
    out = jnp.dot(second, swap_blocks(half, size), preferred_element_type=jnp.float32)
    return out[:size], out[size:]


def multiply(a_real, a_imag, b_real, b_imag):
    return (a_real * b_real - a_imag * b_imag, a_real * b_imag + a_imag * b_real)


def multiply_conj(a_real, a_imag, b_real, b_imag):
    return (a_real * b_real + a_imag * b_imag, a_imag * b_real - a_real * b_imag)


def grads_kernel(
    counts_ref,
    corner_ref,
    own_ref,
    right_ref,
    lower_ref,
    probe_ref,
    prop_ref,
    measured_ref,
    dft_ref,
    grad_ref,
    side_ref,
    foot_ref,
    probe_out_ref,
    ext_ref,
    acc_ref,
    enter_ref,
    probe_acc_ref,
):
    size = probe_ref.shape[-1]
    layers = ext_ref.shape[1]
    pairs = probe_ref.shape[0] // 2
    f32, bf16 = jnp.float32, jnp.bfloat16
    ext_ref[0, :, :, :size] = own_ref[...].astype(f32)
    ext_ref[1, :, :, :size] = right_ref[...].astype(f32)
    ext_ref[0, :, :, size:] = lower_ref[0].astype(f32)
    ext_ref[1, :, :, size:] = lower_ref[1].astype(f32)
    acc_ref[...] = jnp.zeros_like(acc_ref)
    probe_acc_ref[...] = jnp.zeros_like(probe_acc_ref)
    for pair in range(pairs):
        for part in range(2):
            enter_ref[pair, part] = jnp.concatenate(
                [probe_ref[2 * pair, part], probe_ref[2 * pair + 1, part]], 1
            )
    minus, plus = dft_ref[0], dft_ref[1]
    forward = functools.partial(transform, first=minus, second=plus)
    inverse = functools.partial(transform, first=plus, second=minus)

    def twice(block):
        return jnp.concatenate([block, block], 1)

    def fold(block):
        return block[:, :size] + block[:, size:]

    def visit(slot, live):
        row, col = corner_ref[slot, 0], corner_ref[slot, 1]
        patch = [
            [
                twice(
                    pltpu.roll(
                        jnp.concatenate(
                            [ext_ref[side, layer, part, pl.ds(row, size), :] for side in range(2)],
                            1,
                        ),
                        lax.rem(2 * size - col, 2 * size),
                        1,
                    )[:, :size]
                )
                for part in range(2)
            ]
            for layer in range(layers)
        ]
        prop = [twice(prop_ref[part]) for part in range(2)]
        entering = [[(enter_ref[pair, 0], enter_ref[pair, 1]) for pair in range(pairs)]]
        far = [None] * pairs
        for layer in range(layers):
            following = []
            for pair in range(pairs):
                leave = multiply(*entering[layer][pair], *patch[layer])
                freq = forward(*leave)
                if layer < layers - 1:
                    following.append(inverse(*multiply(*freq, *prop)))
                else:
                    far[pair] = freq
            entering.append(following)
        power = sum(real * real + imag * imag for real, imag in far)
        residual = jnp.where(live, fold(power) - measured_ref[slot], 0.0)
        residual = twice(residual)
        back = [inverse(residual * real, residual * imag) for real, imag in far]
        slice_grads = [None] * layers
        to_enter = [None] * pairs
        for layer in reversed(range(layers)):
            terms = [multiply_conj(*back[pair], *entering[layer][pair]) for pair in range(pairs)]
            slice_grads[layer] = [fold(sum(term[part] for term in terms)) for part in range(2)]
            for pair in range(pairs):
                to_enter[pair] = multiply_conj(*back[pair], *patch[layer])
                if layer > 0:
                    freq = forward(*to_enter[pair])
                    back[pair] = inverse(*multiply_conj(*freq, *prop))
        return row, col, slice_grads, to_enter

    def visit_group(group, carry):
        done = []
        for which in range(GROUP):
            slot = group * GROUP + which
            done.append(visit(slot, slot < counts_ref[0]))
        for row, col, slice_grads, _ in done:
            for layer in range(layers):
                for part in range(2):
                    block = slice_grads[layer][part]
                    wide = jnp.concatenate([block, jnp.zeros_like(block)], 1)
                    wide = pltpu.roll(wide, col, 1)
                    rows = pl.ds(row, size)
                    acc_ref[0, layer, part, rows, :] += wide[:, :size]
                    acc_ref[1, layer, part, rows, :] += wide[:, size:]
        for pair in range(pairs):
            for part in range(2):
                probe_acc_ref[pair, part] += sum(entry[3][pair][part] for entry in done)
        return carry

    lax.fori_loop(0, (counts_ref[0] + GROUP - 1) // GROUP, visit_group, 0)
    grad_ref[...] = acc_ref[0, :, :, :size]
    side_ref[0] = acc_ref[1, :, :, :size].astype(bf16)
    side_ref[1] = acc_ref[1, :, :, size:].astype(bf16)
    foot_ref[...] = acc_ref[0, :, :, size:]
    for pair in range(pairs):
        for part in range(2):
            both = probe_acc_ref[pair, part].astype(bf16)
            probe_out_ref[2 * pair, part] = both[:, :size]
            probe_out_ref[2 * pair + 1, part] = both[:, size:]


def local_grads(own, right, lower, probe_modes, prop, measured, dft, counts, corners):
    layers, parts, size, _ = own.shape
    modes = probe_modes.shape[0]
    f32, bf16 = jnp.float32, jnp.bfloat16
    vmem = pl.BlockSpec(memory_space=pltpu.VMEM)
    smem = pl.BlockSpec(memory_space=pltpu.SMEM)
    tile = (layers, parts, size, size)
    return pl.pallas_call(
        grads_kernel,
        out_shape=(
            jax.ShapeDtypeStruct(tile, f32),
            jax.ShapeDtypeStruct((2,) + tile, bf16),
            jax.ShapeDtypeStruct(tile, f32),
            jax.ShapeDtypeStruct(probe_modes.shape, bf16),
        ),
        in_specs=[smem] * 2 + [vmem] * 7,
        out_specs=(vmem,) * 4,
        scratch_shapes=[
            pltpu.VMEM((2, layers, parts, 2 * size, size), f32),
            pltpu.VMEM((2, layers, parts, 2 * size, size), f32),
            pltpu.VMEM((modes // 2, 2, size, 2 * size), f32),
            pltpu.VMEM((modes // 2, 2, size, 2 * size), f32),
        ],
        compiler_params=pltpu.CompilerParams(vmem_limit_bytes=40 * 1024 * 1024),
    )(counts, corners, own, right, lower, probe_modes, prop, measured, dft)


def body(object_slices, probe_modes, prop_phase, measured, counts, coords):
    tile_rows = object_slices.shape[2]
    tile_cols = object_slices.shape[3]
    col_count = lax.axis_size("col")
    origin = jnp.stack([lax.axis_index("row") * tile_rows, lax.axis_index("col") * tile_cols])
    corners = coords - origin.astype(jnp.int32)
    dft = dft_matrices(probe_modes.shape[-1])
    prop = jnp.stack([jnp.cos(prop_phase), jnp.sin(prop_phase)])
    right = from_behind(object_slices, "col", -1)
    lower = from_behind(jnp.stack([object_slices, right]), "row", -1)
    grad, side, foot, probe_part = local_grads(
        object_slices, right, lower, probe_modes, prop, measured, dft, counts, corners
    )
    side_back = from_behind(side, "col", 1).astype(jnp.float32)
    shares = probe_part.reshape(col_count, -1, probe_part.shape[-1])
    received = lax.all_to_all(shares, "col", 0, 0, tiled=True)
    foot_back = from_behind((foot + side_back[1]).astype(jnp.bfloat16), "row", 1)
    share = jnp.sum(received.astype(jnp.float32), 0).astype(jnp.bfloat16)
    spread = lax.all_to_all(
        jnp.broadcast_to(share[None], shares.shape), "col", 0, 0, tiled=True
    )
    owned = grad + side_back[0] + foot_back.astype(jnp.float32)
    region_slots = measured.shape[0] * col_count
    probe_total = spread.reshape(probe_part.shape).astype(jnp.float32)
    return (owned, (probe_total * (1.0 / math.sqrt(region_slots)))[None])


def solution(mesh):
    return jax.shard_map(
        body,
        mesh=mesh,
        in_specs=(
            P(None, None, "row", "col"),
            P(),
            P(),
            P(("row", "col"), None, None),
            P(("row", "col")),
            P(("row", "col"), None),
        ),
        out_specs=(P(None, None, "row", "col"), P("row", None, None, None, None)),
        check_vma=False,
    )
```

time: 133 us -> 77.6 us (0.58)
  the two profiles are of different devices: /device:TPU:16 before, /device:TPU:56 now
where the time goes in v2:
time: 77.6 us; the launch traced here: 76.8 us
  starting transfers between devices  32 us (41%)
  waiting for transfers between devices  26.1 us (34%)
  Pallas kernels  13.7 us (18%)
  other arithmetic  2.42 us (3%)
  between operations  1.44 us (2%)
  local copies, waits for them, and re-layouts  1.12 us (1%)
    ppermute x4, waiting for transfers between devices, from_behind(): return lax.ppermute(block, axis, route)  21.2 us
    pallas_call x1, Pallas kernels, local_grads(): pl.pallas_call(grads_kernel, out_shape=(jax.ShapeDtypeStruct(tile, f32),...  13.7 us
    all_to_all x1, starting transfers between devices, body(): received = lax.all_to_all(shares, 'col', 0, 0, tiled=True)  13.1 us
    ppermute x4, starting transfers between devices, from_behind(): return lax.ppermute(block, axis, route)  10.4 us
    all_to_all x1, starting transfers between devices, body(): lax.all_to_all(jnp.broadcast_to(share[None], shares.shape), 'col', 0, 0,...  8.57 us
    all_to_all x1, waiting for transfers between devices, body(): lax.all_to_all(jnp.broadcast_to(share[None], shares.shape), 'col', 0, 0,...  3.11 us
    all_to_all x1, waiting for transfers between devices, body(): received = lax.all_to_all(shares, 'col', 0, 0, tiled=True)  1.82 us
  transfers between devices with their start and end apart: 6, of which 6 were waited for; matrix products, arithmetic and copies ran while one was open for 2% of the time, Pallas kernels for 0%

profile of v2, /device:TPU:56, one launch (start us, length us, event | category | flops | bytes accessed | tf_op | source)
XLA Modules:
  0.0 76.8 jit_solution(16966185808754564590)
XLA Ops:
  0.6 0.0 copy-start.3
  0.6 1.4 %collective-permute-start = (bf16[2,2,128,128]{3,2,1,0:T(8,128)(2,1)}, bf16[2,2,128,128]{3,2,1,0:T(8,128)(2,1)S(1)}, u32[]{:S(2)}, u32[]{:S(2)}) collective-permute-start(bf16[2,2,128,128]{3,2,1,0:T(8,128)(2,1)} %own_ref.1), channel_id=1, source_target_pairs={{1,0},{2,1},{3,2},{4,3},{5,4},{6,5},{7,6},{8,7},{9,8},{10,9},{11,1... | collective-permute-start | bytes 393224 | tf_op jit(solution)/shard_map/ppermute | solution.py:17
  2.1 0.3 fusion.14
  2.3 0.3 multiply_convert_fusion
  2.6 0.0 copy-done.3
  2.6 0.2 cosine_bitcast_fusion
  2.9 0.0 copy-start.1
  2.9 0.0 copy-start
  3.0 5.8 %collective-permute-done.right_ref = bf16[2,2,128,128]{3,2,1,0:T(8,128)(2,1)S(1)} collective-permute-done((bf16[2,2,128,128]{3,2,1,0:T(8,128)(2,1)}, bf16[2,2,128,128]{3,2,1,0:T(8,128)(2,1)S(1)}, u32[]{:S(2)}, u32[]{:S(2)}) %collective-permute-start) | collective-permute-done | bytes 131104 | tf_op jit(solution)/shard_map/ppermute | solution.py:17
  8.8 0.0 copy-done.1
  8.8 0.0 copy-start.2
  8.8 3.2 %collective-permute-start.1 = (bf16[2,2,2,128,128]{4,3,2,1,0:T(8,128)(2,1)S(1)}, bf16[2,2,2,128,128]{4,3,2,1,0:T(8,128)(2,1)S(1)}, u32[]{:S(2)}, u32[]{:S(2)}) collective-permute-start(bf16[2,2,2,128,128]{4,3,2,1,0:T(8,128)(2,1)S(1)} %pad_maximum_fusion), channel_id=1, source_target_pairs={{16,0},{32,16},{48,32},{64,48},{80,64},{96,80},{112,96},{128,112},... | collective-permute-start | bytes 786440 | tf_op jit(solution)/shard_map/ppermute | solution.py:17
  12.0 0.1 pad_add_fusion
  12.1 0.0 copy-start.4
  12.7 0.0 copy-done.4
  12.8 0.1 copy.8
  12.9 3.0 %collective-permute-done.1.lower_ref = bf16[2,2,2,128,128]{4,3,2,1,0:T(8,128)(2,1)S(1)} collective-permute-done((bf16[2,2,2,128,128]{4,3,2,1,0:T(8,128)(2,1)S(1)}, bf16[2,2,2,128,128]{4,3,2,1,0:T(8,128)(2,1)S(1)}, u32[]{:S(2)}, u32[]{:S(2)}) %collective-permute-start.1) | collective-permute-done | bytes 262176 | tf_op jit(solution)/shard_map/ppermute | solution.py:17
  15.9 0.0 copy-done
  15.9 0.0 copy-done.2
  15.9 13.7 %shard_map.77 = (f32[2,2,128,128]{3,2,1,0:T(8,128)S(1)}, bf16[2,2,2,128,128]{4,3,2,1,0:T(8,128)(2,1)S(1)}, f32[2,2,128,128]{3,2,1,0:T(8,128)S(1)}, bf16[4,2,128,128]{3,2,1,0:T(8,128)(2,1)}) custom-call(s32[1]{0:T(128)S(6)} %copy.9.counts_ref, s32[4,2]{1,0:T(4,128)S(1)} %broadcast_subtract_fusion.corner_ref, bf16[2,2,128,128]{3,2,1,0:T(8,128)(2,1)S(1)} %copy-done.1, ...), custom_call_target="tpu_custom_call" | custom-call | tf_op jit(solution)/shard_map/pallas_call | solution.py:197
  29.5 13.1 %all-to-all-start = ((bf16[16,64,128]{2,1,0:T(8,128)(2,1)}), bf16[16,64,128]{2,1,0:T(8,128)(2,1)S(1)}, u32[]{:S(2)}, u32[]{:S(2)}) async-start(bf16[16,64,128]{2,1,0:T(8,128)(2,1)} %bitcast.10), calls=%async_computation | async-start | bytes 524288 | tf_op jit(solution)/shard_map/all_to_all | solution.py:232
  42.6 3.8 %collective-permute-start.2 = (bf16[2,2,2,128,128]{4,3,2,1,0:T(8,128)(2,1)S(1)}, bf16[2,2,2,128,128]{4,3,2,1,0:T(8,128)(2,1)S(1)}, u32[]{:S(2)}, u32[]{:S(2)}) collective-permute-start(bf16[2,2,2,128,128]{4,3,2,1,0:T(8,128)(2,1)S(1)} %get-tuple-element.7), channel_id=1, source_target_pairs={{0,1},{1,2},{2,3},{3,4},{4,5},{5,6},{6,7},{7,8},{8,9},{9,10},{10,1... | collective-permute-start | bytes 786440 | tf_op jit(solution)/shard_map/ppermute | solution.py:17
  46.4 7.2 %collective-permute-done.2 = bf16[2,2,2,128,128]{4,3,2,1,0:T(8,128)(2,1)S(1)} collective-permute-done((bf16[2,2,2,128,128]{4,3,2,1,0:T(8,128)(2,1)S(1)}, bf16[2,2,2,128,128]{4,3,2,1,0:T(8,128)(2,1)S(1)}, u32[]{:S(2)}, u32[]{:S(2)}) %collective-permute-start.2) | collective-permute-done | bytes 262176 | tf_op jit(solution)/shard_map/ppermute | solution.py:17
  53.6 1.8 %all-to-all-done = bf16[16,64,128]{2,1,0:T(8,128)(2,1)S(1)} async-done(((bf16[16,64,128]{2,1,0:T(8,128)(2,1)}), bf16[16,64,128]{2,1,0:T(8,128)(2,1)S(1)}, u32[]{:S(2)}, u32[]{:S(2)}) %all-to-all-start) | async-done | bytes 262176 | tf_op jit(solution)/shard_map/all_to_all | solution.py:232
  55.5 0.8 broadcast_in_dim.2
  56.3 8.6 %all-to-all-start.1 = ((bf16[16,64,128]{2,1,0:T(8,128)(2,1)}), bf16[16,64,128]{2,1,0:T(8,128)(2,1)S(1)}, u32[]{:S(2)}, u32[]{:S(2)}) async-start(bf16[16,64,128]{2,1,0:T(8,128)(2,1)} %broadcast_in_dim.2), calls=%async_computation.1 | async-start | bytes 524288 | tf_op jit(solution)/shard_map/all_to_all | solution.py:235
  64.9 1.9 %collective-permute-start.3 = (bf16[2,2,128,128]{3,2,1,0:T(8,128)(2,1)S(1)}, bf16[2,2,128,128]{3,2,1,0:T(8,128)(2,1)S(1)}, u32[]{:S(2)}, u32[]{:S(2)}) collective-permute-start(bf16[2,2,128,128]{3,2,1,0:T(8,128)(2,1)S(1)} %fusion.1), channel_id=1, source_target_pairs={{0,16},{16,32},{32,48},{48,64},{64,80},{80,96},{96,112},{112,128},... | collective-permute-start | bytes 393224 | tf_op jit(solution)/shard_map/ppermute | solution.py:17
  66.8 5.3 %collective-permute-done.3 = bf16[2,2,128,128]{3,2,1,0:T(8,128)(2,1)S(1)} collective-permute-done((bf16[2,2,128,128]{3,2,1,0:T(8,128)(2,1)S(1)}, bf16[2,2,128,128]{3,2,1,0:T(8,128)(2,1)S(1)}, u32[]{:S(2)}, u32[]{:S(2)}) %collective-permute-start.3) | collective-permute-done | bytes 131104 | tf_op jit(solution)/shard_map/ppermute | solution.py:17
  72.1 0.7 fusion.3
  72.8 3.1 %all-to-all-done.1 = bf16[16,64,128]{2,1,0:T(8,128)(2,1)S(1)} async-done(((bf16[16,64,128]{2,1,0:T(8,128)(2,1)}), bf16[16,64,128]{2,1,0:T(8,128)(2,1)S(1)}, u32[]{:S(2)}, u32[]{:S(2)}) %all-to-all-start.1) | async-done | bytes 262176 | tf_op jit(solution)/shard_map/all_to_all | solution.py:235
  75.9 0.8 %convert_multiply_fusion = f32[16,64,128]{2,1,0:T(8,128)} fusion(bf16[16,64,128]{2,1,0:T(8,128)(2,1)S(1)} %all-to-all-done.1), kind=kLoop, calls=%fused_computation | loop fusion | flops 262144 | bytes 786432 | tf_op jit(solution)/shard_map/mul | solution.py:241
  (8 shorter events, 0.2 us)
Async XLA Ops:
  0.6 2.0 %copy-start.3 = (f32[128,128]{1,0:T(8,128)S(1)}, f32[128,128]{1,0:T(8,128)}, u32[]{:S(2)}) copy-start(f32[128,128]{1,0:T(8,128)} %param.8) | copy-start | bytes 196612
  0.6 8.1 %collective-permute-start = (bf16[2,2,128,128]{3,2,1,0:T(8,128)(2,1)}, bf16[2,2,128,128]{3,2,1,0:T(8,128)(2,1)S(1)}, u32[]{:S(2)}, u32[]{:S(2)}) collective-permute-start(bf16[2,2,128,128]{3,2,1,0:T(8,128)(2,1)} %own_ref.1), channel_id=1, source_target_pairs={{1,0},{2,1},{3,2},{4,3},{5,4},{6,5},{7,6},{8,7},{9,8},{10,9},{11,1... | collective-permute-start | bytes 393224 | tf_op jit(solution)/shard_map/ppermute | solution.py:17
  2.9 5.8 %copy-start.1 = (bf16[2,2,128,128]{3,2,1,0:T(8,128)(2,1)S(1)}, bf16[2,2,128,128]{3,2,1,0:T(8,128)(2,1)}, u32[]{:S(2)}) copy-start(bf16[2,2,128,128]{3,2,1,0:T(8,128)(2,1)} %own_ref.1) | copy-start | bytes 393220
  2.9 12.9 %copy-start = (f32[4,2,128,128]{3,2,1,0:T(8,128)S(1)}, f32[4,2,128,128]{3,2,1,0:T(8,128)}, u32[]{:S(2)}) copy-start(f32[4,2,128,128]{3,2,1,0:T(8,128)} %probe_ref.1) | copy-start | bytes 1572868
  8.8 7.1 %copy-start.2 = (f32[4,128,128]{2,1,0:T(8,128)S(1)}, f32[4,128,128]{2,1,0:T(8,128)}, u32[]{:S(2)}) copy-start(f32[4,128,128]{2,1,0:T(8,128)} %measured_ref.1) | copy-start | bytes 786436
  8.8 7.1 %collective-permute-start.1 = (bf16[2,2,2,128,128]{4,3,2,1,0:T(8,128)(2,1)S(1)}, bf16[2,2,2,128,128]{4,3,2,1,0:T(8,128)(2,1)S(1)}, u32[]{:S(2)}, u32[]{:S(2)}) collective-permute-start(bf16[2,2,2,128,128]{4,3,2,1,0:T(8,128)(2,1)S(1)} %pad_maximum_fusion), channel_id=1, source_target_pairs={{16,0},{32,16},{48,32},{64,48},{80,64},{96,80},{112,96},{128,112},... | collective-permute-start | bytes 786440 | tf_op jit(solution)/shard_map/ppermute | solution.py:17
  12.1 0.7 copy-start.4
  29.5 25.9 %all-to-all-start = ((bf16[16,64,128]{2,1,0:T(8,128)(2,1)}), bf16[16,64,128]{2,1,0:T(8,128)(2,1)S(1)}, u32[]{:S(2)}, u32[]{:S(2)}) async-start(bf16[16,64,128]{2,1,0:T(8,128)(2,1)} %bitcast.10), calls=%async_computation | async-start | bytes 524288 | tf_op jit(solution)/shard_map/all_to_all | solution.py:232
  42.6 11.0 %collective-permute-start.2 = (bf16[2,2,2,128,128]{4,3,2,1,0:T(8,128)(2,1)S(1)}, bf16[2,2,2,128,128]{4,3,2,1,0:T(8,128)(2,1)S(1)}, u32[]{:S(2)}, u32[]{:S(2)}) collective-permute-start(bf16[2,2,2,128,128]{4,3,2,1,0:T(8,128)(2,1)S(1)} %get-tuple-element.7), channel_id=1, source_target_pairs={{0,1},{1,2},{2,3},{3,4},{4,5},{5,6},{6,7},{7,8},{8,9},{9,10},{10,1... | collective-permute-start | bytes 786440 | tf_op jit(solution)/shard_map/ppermute | solution.py:17
  56.3 19.7 %all-to-all-start.1 = ((bf16[16,64,128]{2,1,0:T(8,128)(2,1)}), bf16[16,64,128]{2,1,0:T(8,128)(2,1)S(1)}, u32[]{:S(2)}, u32[]{:S(2)}) async-start(bf16[16,64,128]{2,1,0:T(8,128)(2,1)} %broadcast_in_dim.2), calls=%async_computation.1 | async-start | bytes 524288 | tf_op jit(solution)/shard_map/all_to_all | solution.py:235
  64.9 7.2 %collective-permute-start.3 = (bf16[2,2,128,128]{3,2,1,0:T(8,128)(2,1)S(1)}, bf16[2,2,128,128]{3,2,1,0:T(8,128)(2,1)S(1)}, u32[]{:S(2)}, u32[]{:S(2)}) collective-permute-start(bf16[2,2,128,128]{3,2,1,0:T(8,128)(2,1)S(1)} %fusion.1), channel_id=1, source_target_pairs={{0,16},{16,32},{32,48},{48,64},{64,80},{80,96},{96,112},{112,128},... | collective-permute-start | bytes 393224 | tf_op jit(solution)/shard_map/ppermute | solution.py:17

commit v3 on v2

v3 whole, which is shorter than its diff:
```python
import functools
import math

import jax
import jax.numpy as jnp
from jax import lax
from jax.experimental import pallas as pl
from jax.experimental.pallas import tpu as pltpu
from jax.sharding import PartitionSpec as P


def from_behind(block, axis, distance):
    devices = range(lax.axis_size(axis))
    route = [(i - distance, i) for i in devices if i - distance in devices]
    return lax.ppermute(block, axis, route)


def dft_matrices(size):
    steps_idx = jnp.arange(size, dtype=jnp.int32)
    product_idx = steps_idx[:, None] * steps_idx[None, :] % size
    angle = product_idx.astype(jnp.float32) * (2.0 * math.pi / size)
    scale = 1.0 / math.sqrt(size)
    cos_table = (jnp.cos(angle) * scale).astype(jnp.bfloat16)
    sin_table = (jnp.sin(angle) * scale).astype(jnp.bfloat16)
    minus = jnp.concatenate(
        [
            jnp.concatenate([cos_table, -sin_table], 1),
            jnp.concatenate([sin_table, cos_table], 1),
        ],
        0,
    )
    plus = jnp.concatenate(
        [
            jnp.concatenate([cos_table, sin_table], 1),
            jnp.concatenate([-sin_table, cos_table], 1),
        ],
        0,
    )
    return jnp.stack([minus, plus])


def swap_blocks(matrix, size):
    upper = jnp.concatenate([matrix[:size, :size], matrix[size:, :size]], 1)
    lower = jnp.concatenate([matrix[:size, size:], matrix[size:, size:]], 1)
    return jnp.concatenate([upper, lower], 0)


def transform(waves, first, second):
    size = waves[0][0].shape[0]
    stacked = [
        swap_blocks(jnp.concatenate([real, imag], 0).astype(jnp.bfloat16), size)
        for real, imag in waves
    ]
    halves = first_stage(stacked, first)
    outs = second_stage([swap_blocks(half, size) for half in halves], second)
    return [(out[:size], out[size:]) for out in outs]


def first_stage(stacked, first):
    rows = stacked[0].shape[0]
    half = jnp.dot(
        jnp.concatenate(stacked, 0), first, preferred_element_type=jnp.float32
    ).astype(jnp.bfloat16)
    return [half[i * rows : (i + 1) * rows] for i in range(len(stacked))]


def second_stage(halves, second):
    cols = halves[0].shape[1]
    out = jnp.dot(second, jnp.concatenate(halves, 1), preferred_element_type=jnp.float32)
    return [out[:, i * cols : (i + 1) * cols] for i in range(len(halves))]


def multiply(a_real, a_imag, b_real, b_imag):
    return (a_real * b_real - a_imag * b_imag, a_real * b_imag + a_imag * b_real)


def multiply_conj(a_real, a_imag, b_real, b_imag):
    return (a_real * b_real + a_imag * b_imag, a_imag * b_real - a_real * b_imag)


def grads_kernel(
    counts_ref,
    corner_ref,
    own_ref,
    right_ref,
    lower_ref,
    probe_ref,
    prop_ref,
    measured_ref,
    dft_ref,
    grad_ref,
    side_ref,
    foot_ref,
    probe_out_ref,
    ext_ref,
    acc_ref,
):
    size = probe_ref.shape[-1]
    layers = ext_ref.shape[1]
    pairs = probe_ref.shape[0] // 2
    f32, bf16 = jnp.float32, jnp.bfloat16
    ext_ref[0, :, :, :size] = own_ref[...].astype(f32)
    ext_ref[1, :, :, :size] = right_ref[...].astype(f32)
    ext_ref[0, :, :, size:] = lower_ref[0].astype(f32)
    ext_ref[1, :, :, size:] = lower_ref[1].astype(f32)
    acc_ref[...] = jnp.zeros_like(acc_ref)
    minus, plus = dft_ref[0], dft_ref[1]
    forward = functools.partial(transform, first=minus, second=plus)
    inverse = functools.partial(transform, first=plus, second=minus)

    def twice(block):
        return jnp.concatenate([block, block], 1)

    def fold(block):
        return block[:, :size] + block[:, size:]

    def load_patch(row, col, layer, part):
        rows = pl.ds(row, size)
        both = jnp.concatenate([ext_ref[side, layer, part, rows, :] for side in range(2)], 1)
        return twice(pltpu.roll(both, lax.rem(2 * size - col, 2 * size), 1)[:, :size])

    slots = range(measured_ref.shape[0])
    corners = [(corner_ref[slot, 0], corner_ref[slot, 1]) for slot in slots]
    patches = [
        [[load_patch(row, col, layer, part) for part in range(2)] for layer in range(layers)]
        for row, col in corners
    ]
    units = [(which, pair) for which in slots for pair in range(pairs)]
    prop = [twice(prop_ref[part]) for part in range(2)]
    probe = [
        tuple(
            jnp.concatenate([probe_ref[2 * pair, part], probe_ref[2 * pair + 1, part]], 1)
            for part in range(2)
        )
        for pair in range(pairs)
    ]
    entering = [[probe[pair] for _, pair in units]]
    for layer in range(layers):
        leaving = [
            multiply(*wave, *patches[which][layer])
            for wave, (which, _) in zip(entering[layer], units)
        ]
        freqs = forward(leaving)
        if layer < layers - 1:
            entering.append(inverse([multiply(*freq, *prop) for freq in freqs]))
    far = freqs
    residuals = []
    for which, slot in enumerate(slots):
        power = sum(
            real * real + imag * imag
            for (real, imag), unit in zip(far, units)
            if unit[0] == which
        )
        residual = jnp.where(slot < counts_ref[0], fold(power) - measured_ref[slot], 0.0)
        residuals.append(twice(residual))
    back = inverse(
        [
            (residuals[which] * real, residuals[which] * imag)
            for (real, imag), (which, _) in zip(far, units)
        ]
    )
    for layer in reversed(range(layers)):
        terms = [
            multiply_conj(*wave, *entered) for wave, entered in zip(back, entering[layer])
        ]
        for which, (row, col) in enumerate(corners):
            for part in range(2):
                block = fold(
                    sum(term[part] for term, unit in zip(terms, units) if unit[0] == which)
                )
                wide = jnp.concatenate([block, jnp.zeros_like(block)], 1)
                wide = pltpu.roll(wide, col, 1)
                rows = pl.ds(row, size)
                acc_ref[0, layer, part, rows, :] += wide[:, :size]
                acc_ref[1, layer, part, rows, :] += wide[:, size:]
        to_enter = [
            multiply_conj(*wave, *patches[which][layer])
            for wave, (which, _) in zip(back, units)
        ]
        if layer > 0:
            back = inverse([multiply_conj(*freq, *prop) for freq in forward(to_enter)])
    for pair in range(pairs):
        for part in range(2):
            both = sum(wave[part] for wave, unit in zip(to_enter, units) if unit[1] == pair)
            both = both.astype(bf16)
            probe_out_ref[2 * pair, part] = both[:, :size]
            probe_out_ref[2 * pair + 1, part] = both[:, size:]
    grad_ref[...] = acc_ref[0, :, :, :size]
    side_ref[0] = acc_ref[1, :, :, :size].astype(bf16)
    side_ref[1] = acc_ref[1, :, :, size:].astype(bf16)
    foot_ref[...] = acc_ref[0, :, :, size:]


def local_grads(own, right, lower, probe_modes, prop, measured, dft, counts, corners):
    layers, parts, size, _ = own.shape
    f32, bf16 = jnp.float32, jnp.bfloat16
    vmem = pl.BlockSpec(memory_space=pltpu.VMEM)
    smem = pl.BlockSpec(memory_space=pltpu.SMEM)
    tile = (layers, parts, size, size)
    return pl.pallas_call(
        grads_kernel,
        out_shape=(
            jax.ShapeDtypeStruct(tile, f32),
            jax.ShapeDtypeStruct((2,) + tile, bf16),
            jax.ShapeDtypeStruct(tile, f32),
            jax.ShapeDtypeStruct(probe_modes.shape, bf16),
        ),
        in_specs=[smem] * 2 + [vmem] * 7,
        out_specs=(vmem,) * 4,
        scratch_shapes=[
            pltpu.VMEM((2, layers, parts, 2 * size, size), f32),
            pltpu.VMEM((2, layers, parts, 2 * size, size), f32),
        ],
        compiler_params=pltpu.CompilerParams(vmem_limit_bytes=40 * 1024 * 1024),
    )(counts, corners, own, right, lower, probe_modes, prop, measured, dft)


def body(object_slices, probe_modes, prop_phase, measured, counts, coords):
    tile_rows = object_slices.shape[2]
    tile_cols = object_slices.shape[3]
    col_count = lax.axis_size("col")
    origin = jnp.stack([lax.axis_index("row") * tile_rows, lax.axis_index("col") * tile_cols])
    corners = coords - origin.astype(jnp.int32)
    dft = dft_matrices(probe_modes.shape[-1])
    prop = jnp.stack([jnp.cos(prop_phase), jnp.sin(prop_phase)])
    right = from_behind(object_slices, "col", -1)
    lower = from_behind(jnp.stack([object_slices, right]), "row", -1)
    grad, side, foot, probe_part = local_grads(
        object_slices, right, lower, probe_modes, prop, measured, dft, counts, corners
    )
    side_back = from_behind(side, "col", 1).astype(jnp.float32)
    shares = probe_part.reshape(col_count, -1, probe_part.shape[-1])
    received = lax.all_to_all(shares, "col", 0, 0, tiled=True)
    foot_back = from_behind((foot + side_back[1]).astype(jnp.bfloat16), "row", 1)
    received, foot_back = lax.optimization_barrier((received, foot_back))
    share = jnp.sum(received.astype(jnp.float32), 0).astype(jnp.bfloat16)
    spread = lax.all_to_all(
        jnp.broadcast_to(share[None], shares.shape), "col", 0, 0, tiled=True
    )
    owned = grad + side_back[0] + foot_back.astype(jnp.float32)
    region_slots = measured.shape[0] * col_count
    probe_total = spread.reshape(probe_part.shape).astype(jnp.float32)
    return (owned, (probe_total * (1.0 / math.sqrt(region_slots)))[None])


def solution(mesh):
    return jax.shard_map(
        body,
        mesh=mesh,
        in_specs=(
            P(None, None, "row", "col"),
            P(),
            P(),
            P(("row", "col"), None, None),
            P(("row", "col")),
            P(("row", "col"), None),
        ),
        out_specs=(P(None, None, "row", "col"), P("row", None, None, None, None)),
        check_vma=False,
    )
```

time: 77.6 us -> 69.9 us (0.901)
  Pallas kernels: 13.7 us -> 6.34 us
  starting transfers between devices: 32 us -> 28 us
  waiting for transfers between devices: 26.1 us -> 29.8 us
    all_to_all x1, waiting for transfers between devices: 3.11 us -> 11 us  [body(): lax.all_to_all(jnp.broadcast_to(share[None], shares.shape), 'col', 0, 0,...]
    pallas_call x1, Pallas kernels: 13.7 us -> 6.34 us  [local_grads(): pl.pallas_call(grads_kernel, out_shape=(jax.ShapeDtypeStruct(tile, f32),...]
    ppermute x4, waiting for transfers between devices: 21.2 us -> 13.9 us  [from_behind(): return lax.ppermute(block, axis, route)]
    all_to_all x1, starting transfers between devices: 8.57 us -> 4.61 us  [body(): lax.all_to_all(jnp.broadcast_to(share[None], shares.shape), 'col', 0, 0,...]
    all_to_all x1, waiting for transfers between devices: 1.82 us -> 4.82 us  [body(): received = lax.all_to_all(shares, 'col', 0, 0, tiled=True)]
    all_to_all x1, starting transfers between devices: 13.1 us -> 12.2 us  [body(): received = lax.all_to_all(shares, 'col', 0, 0, tiled=True)]
    ppermute x4, starting transfers between devices: 10.4 us -> 11.2 us  [from_behind(): return lax.ppermute(block, axis, route)]
  transfers between devices with their start and end apart: 6 -> 6, of which waited for: 6 -> 5; matrix products, arithmetic and copies ran while one was open for 2% -> 3% of each run, Pallas kernels for 0% -> 0%
where the time goes in v3:
time: 69.9 us; the launch traced here: 69.1 us
  waiting for transfers between devices  29.8 us (43%)
  starting transfers between devices  28 us (40%)
  Pallas kernels  6.34 us (9%)
  other arithmetic  2.42 us (3%)
  between operations  1.45 us (2%)
  local copies, waits for them, and re-layouts  1.12 us (2%)
    ppermute x4, waiting for transfers between devices, from_behind(): return lax.ppermute(block, axis, route)  13.9 us
    all_to_all x1, starting transfers between devices, body(): received = lax.all_to_all(shares, 'col', 0, 0, tiled=True)  12.2 us
    ppermute x4, starting transfers between devices, from_behind(): return lax.ppermute(block, axis, route)  11.2 us
    all_to_all x1, waiting for transfers between devices, body(): lax.all_to_all(jnp.broadcast_to(share[None], shares.shape), 'col', 0, 0,...  11 us
    pallas_call x1, Pallas kernels, local_grads(): pl.pallas_call(grads_kernel, out_shape=(jax.ShapeDtypeStruct(tile, f32),...  6.34 us
    all_to_all x1, waiting for transfers between devices, body(): received = lax.all_to_all(shares, 'col', 0, 0, tiled=True)  4.82 us
    all_to_all x1, starting transfers between devices, body(): lax.all_to_all(jnp.broadcast_to(share[None], shares.shape), 'col', 0, 0,...  4.61 us
  transfers between devices with their start and end apart: 6, of which 5 were waited for; matrix products, arithmetic and copies ran while one was open for 3% of the time, Pallas kernels for 0%

profile of v3, /device:TPU:56, one launch (start us, length us, event | category | flops | bytes accessed | tf_op | source)
XLA Modules:
  0.0 69.1 jit_solution(5293420300805551972)
XLA Ops:
  0.6 0.0 copy-start.3
  0.6 1.4 %collective-permute-start = (bf16[2,2,128,128]{3,2,1,0:T(8,128)(2,1)}, bf16[2,2,128,128]{3,2,1,0:T(8,128)(2,1)S(1)}, u32[]{:S(2)}, u32[]{:S(2)}) collective-permute-start(bf16[2,2,128,128]{3,2,1,0:T(8,128)(2,1)} %own_ref.1), channel_id=1, source_target_pairs={{1,0},{2,1},{3,2},{4,3},{5,4},{6,5},{7,6},{8,7},{9,8},{10,9},{11,1... | collective-permute-start | bytes 393224 | tf_op jit(solution)/shard_map/ppermute | solution.py:15
  2.1 0.3 fusion.14
  2.3 0.3 multiply_convert_fusion
  2.6 0.0 copy-done.3
  2.6 0.2 cosine_bitcast_fusion
  2.9 0.0 copy-start.1
  2.9 0.0 copy-start
  3.0 5.8 %collective-permute-done.right_ref = bf16[2,2,128,128]{3,2,1,0:T(8,128)(2,1)S(1)} collective-permute-done((bf16[2,2,128,128]{3,2,1,0:T(8,128)(2,1)}, bf16[2,2,128,128]{3,2,1,0:T(8,128)(2,1)S(1)}, u32[]{:S(2)}, u32[]{:S(2)}) %collective-permute-start) | collective-permute-done | bytes 131104 | tf_op jit(solution)/shard_map/ppermute | solution.py:15
  8.8 0.0 copy-done.1
  8.8 0.0 copy-start.2
  8.8 3.2 %collective-permute-start.1 = (bf16[2,2,2,128,128]{4,3,2,1,0:T(8,128)(2,1)S(1)}, bf16[2,2,2,128,128]{4,3,2,1,0:T(8,128)(2,1)S(1)}, u32[]{:S(2)}, u32[]{:S(2)}) collective-permute-start(bf16[2,2,2,128,128]{4,3,2,1,0:T(8,128)(2,1)S(1)} %pad_maximum_fusion), channel_id=1, source_target_pairs={{16,0},{32,16},{48,32},{64,48},{80,64},{96,80},{112,96},{128,112},... | collective-permute-start | bytes 786440 | tf_op jit(solution)/shard_map/ppermute | solution.py:15
  12.0 0.1 pad_add_fusion
  12.1 0.0 copy-start.4
  12.7 0.0 copy-done.4
  12.8 0.1 copy.8
  12.9 3.0 %collective-permute-done.1.lower_ref = bf16[2,2,2,128,128]{4,3,2,1,0:T(8,128)(2,1)S(1)} collective-permute-done((bf16[2,2,2,128,128]{4,3,2,1,0:T(8,128)(2,1)S(1)}, bf16[2,2,2,128,128]{4,3,2,1,0:T(8,128)(2,1)S(1)}, u32[]{:S(2)}, u32[]{:S(2)}) %collective-permute-start.1) | collective-permute-done | bytes 262176 | tf_op jit(solution)/shard_map/ppermute | solution.py:15
  15.9 0.0 copy-done
  15.9 0.0 copy-done.2
  15.9 6.3 %shard_map.77 = (f32[2,2,128,128]{3,2,1,0:T(8,128)S(1)}, bf16[2,2,2,128,128]{4,3,2,1,0:T(8,128)(2,1)S(1)}, f32[2,2,128,128]{3,2,1,0:T(8,128)S(1)}, bf16[4,2,128,128]{3,2,1,0:T(8,128)(2,1)}) custom-call(s32[1]{0:T(128)S(6)} %copy.9.counts_ref, s32[4,2]{1,0:T(4,128)S(1)} %broadcast_subtract_fusion.corner_ref, bf16[2,2,128,128]{3,2,1,0:T(8,128)(2,1)S(1)} %copy-done.1, ...), custom_call_target="tpu_custom_call" | custom-call | tf_op jit(solution)/shard_map/pallas_call | solution.py:200
  22.2 4.3 %collective-permute-start.2 = (bf16[2,2,2,128,128]{4,3,2,1,0:T(8,128)(2,1)S(1)}, bf16[2,2,2,128,128]{4,3,2,1,0:T(8,128)(2,1)S(1)}, u32[]{:S(2)}, u32[]{:S(2)}) collective-permute-start(bf16[2,2,2,128,128]{4,3,2,1,0:T(8,128)(2,1)S(1)} %get-tuple-element.9), channel_id=1, source_target_pairs={{0,1},{1,2},{2,3},{3,4},{4,5},{5,6},{6,7},{7,8},{8,9},{9,10},{10,1... | collective-permute-start | bytes 786440 | tf_op jit(solution)/shard_map/ppermute | solution.py:15
  26.5 12.2 %all-to-all-start = ((bf16[16,64,128]{2,1,0:T(8,128)(2,1)}), bf16[16,64,128]{2,1,0:T(8,128)(2,1)S(1)}, u32[]{:S(2)}, u32[]{:S(2)}) async-start(bf16[16,64,128]{2,1,0:T(8,128)(2,1)} %bitcast.9), calls=%async_computation | async-start | bytes 524288 | tf_op jit(solution)/shard_map/all_to_all | solution.py:233
  38.7 0.0 collective-permute-done.2
  38.8 2.3 %collective-permute-start.3 = (bf16[2,2,128,128]{3,2,1,0:T(8,128)(2,1)S(1)}, bf16[2,2,128,128]{3,2,1,0:T(8,128)(2,1)S(1)}, u32[]{:S(2)}, u32[]{:S(2)}) collective-permute-start(bf16[2,2,128,128]{3,2,1,0:T(8,128)(2,1)S(1)} %fusion.1), channel_id=1, source_target_pairs={{0,16},{16,32},{32,48},{48,64},{64,80},{80,96},{96,112},{112,128},... | collective-permute-start | bytes 393224 | tf_op jit(solution)/shard_map/ppermute | solution.py:15
  41.1 5.2 %collective-permute-done.3 = bf16[2,2,128,128]{3,2,1,0:T(8,128)(2,1)S(1)} collective-permute-done((bf16[2,2,128,128]{3,2,1,0:T(8,128)(2,1)S(1)}, bf16[2,2,128,128]{3,2,1,0:T(8,128)(2,1)S(1)}, u32[]{:S(2)}, u32[]{:S(2)}) %collective-permute-start.3) | collective-permute-done | bytes 131104 | tf_op jit(solution)/shard_map/ppermute | solution.py:15
  46.3 4.8 %all-to-all-done = bf16[16,64,128]{2,1,0:T(8,128)(2,1)S(1)} async-done(((bf16[16,64,128]{2,1,0:T(8,128)(2,1)}), bf16[16,64,128]{2,1,0:T(8,128)(2,1)S(1)}, u32[]{:S(2)}, u32[]{:S(2)}) %all-to-all-start) | async-done | bytes 262176 | tf_op jit(solution)/shard_map/all_to_all | solution.py:233
  51.1 0.8 %broadcast_in_dim.2 = bf16[16,64,128]{2,1,0:T(8,128)(2,1)} broadcast(bf16[64,128]{1,0:T(8,128)(2,1)S(1)} %reduce_sum.12), dimensions={1,2} | broadcast | bytes 278528 | tf_op jit(solution)/shard_map/broadcast_in_dim | solution.py:238
  51.9 4.6 %all-to-all-start.1 = ((bf16[16,64,128]{2,1,0:T(8,128)(2,1)}), bf16[16,64,128]{2,1,0:T(8,128)(2,1)S(1)}, u32[]{:S(2)}, u32[]{:S(2)}) async-start(bf16[16,64,128]{2,1,0:T(8,128)(2,1)} %broadcast_in_dim.2), calls=%async_computation.1 | async-start | bytes 524288 | tf_op jit(solution)/shard_map/all_to_all | solution.py:237
  56.5 0.7 %fusion.3 = f32[2,2,128,128]{3,2,1,0:T(8,128)} fusion(f32[2,2,128,128]{3,2,1,0:T(8,128)S(1)} %get-tuple-element.8, f32[2,2,2,128,128]{4,3,2,1,0:T(8,128)S(1)} %convert_element_type.60, bf16[2,2,128,128]{3,2,1,0:T(8,128)(2,1)S(1)} %collective-permute-done.3), kind=kLoop, calls=%fused_computation.6 | loop fusion | flops 196608 | bytes 917504 | tf_op jit(solution)/shard_map/add | solution.py:240
  57.3 11.0 %all-to-all-done.1 = bf16[16,64,128]{2,1,0:T(8,128)(2,1)S(1)} async-done(((bf16[16,64,128]{2,1,0:T(8,128)(2,1)}), bf16[16,64,128]{2,1,0:T(8,128)(2,1)S(1)}, u32[]{:S(2)}, u32[]{:S(2)}) %all-to-all-start.1) | async-done | bytes 262176 | tf_op jit(solution)/shard_map/all_to_all | solution.py:237
  68.3 0.8 %convert_multiply_fusion = f32[16,64,128]{2,1,0:T(8,128)} fusion(bf16[16,64,128]{2,1,0:T(8,128)(2,1)S(1)} %all-to-all-done.1), kind=kLoop, calls=%fused_computation | loop fusion | flops 262144 | bytes 786432 | tf_op jit(solution)/shard_map/mul | solution.py:243
  (8 shorter events, 0.2 us)
Async XLA Ops:
  0.6 2.0 %copy-start.3 = (f32[128,128]{1,0:T(8,128)S(1)}, f32[128,128]{1,0:T(8,128)}, u32[]{:S(2)}) copy-start(f32[128,128]{1,0:T(8,128)} %param.8) | copy-start | bytes 196612
  0.6 8.1 %collective-permute-start = (bf16[2,2,128,128]{3,2,1,0:T(8,128)(2,1)}, bf16[2,2,128,128]{3,2,1,0:T(8,128)(2,1)S(1)}, u32[]{:S(2)}, u32[]{:S(2)}) collective-permute-start(bf16[2,2,128,128]{3,2,1,0:T(8,128)(2,1)} %own_ref.1), channel_id=1, source_target_pairs={{1,0},{2,1},{3,2},{4,3},{5,4},{6,5},{7,6},{8,7},{9,8},{10,9},{11,1... | collective-permute-start | bytes 393224 | tf_op jit(solution)/shard_map/ppermute | solution.py:15
  2.9 5.8 %copy-start.1 = (bf16[2,2,128,128]{3,2,1,0:T(8,128)(2,1)S(1)}, bf16[2,2,128,128]{3,2,1,0:T(8,128)(2,1)}, u32[]{:S(2)}) copy-start(bf16[2,2,128,128]{3,2,1,0:T(8,128)(2,1)} %own_ref.1) | copy-start | bytes 393220
  2.9 12.9 %copy-start = (f32[4,2,128,128]{3,2,1,0:T(8,128)S(1)}, f32[4,2,128,128]{3,2,1,0:T(8,128)}, u32[]{:S(2)}) copy-start(f32[4,2,128,128]{3,2,1,0:T(8,128)} %probe_ref.1) | copy-start | bytes 1572868
  8.8 7.1 %copy-start.2 = (f32[4,128,128]{2,1,0:T(8,128)S(1)}, f32[4,128,128]{2,1,0:T(8,128)}, u32[]{:S(2)}) copy-start(f32[4,128,128]{2,1,0:T(8,128)} %measured_ref.1) | copy-start | bytes 786436
  8.8 7.1 %collective-permute-start.1 = (bf16[2,2,2,128,128]{4,3,2,1,0:T(8,128)(2,1)S(1)}, bf16[2,2,2,128,128]{4,3,2,1,0:T(8,128)(2,1)S(1)}, u32[]{:S(2)}, u32[]{:S(2)}) collective-permute-start(bf16[2,2,2,128,128]{4,3,2,1,0:T(8,128)(2,1)S(1)} %pad_maximum_fusion), channel_id=1, source_target_pairs={{16,0},{32,16},{48,32},{64,48},{80,64},{96,80},{112,96},{128,112},... | collective-permute-start | bytes 786440 | tf_op jit(solution)/shard_map/ppermute | solution.py:15
  12.1 0.7 copy-start.4
  22.2 16.5 %collective-permute-start.2 = (bf16[2,2,2,128,128]{4,3,2,1,0:T(8,128)(2,1)S(1)}, bf16[2,2,2,128,128]{4,3,2,1,0:T(8,128)(2,1)S(1)}, u32[]{:S(2)}, u32[]{:S(2)}) collective-permute-start(bf16[2,2,2,128,128]{4,3,2,1,0:T(8,128)(2,1)S(1)} %get-tuple-element.9), channel_id=1, source_target_pairs={{0,1},{1,2},{2,3},{3,4},{4,5},{5,6},{6,7},{7,8},{8,9},{9,10},{10,1... | collective-permute-start | bytes 786440 | tf_op jit(solution)/shard_map/ppermute | solution.py:15
  26.5 24.6 %all-to-all-start = ((bf16[16,64,128]{2,1,0:T(8,128)(2,1)}), bf16[16,64,128]{2,1,0:T(8,128)(2,1)S(1)}, u32[]{:S(2)}, u32[]{:S(2)}) async-start(bf16[16,64,128]{2,1,0:T(8,128)(2,1)} %bitcast.9), calls=%async_computation | async-start | bytes 524288 | tf_op jit(solution)/shard_map/all_to_all | solution.py:233
  38.8 7.5 %collective-permute-start.3 = (bf16[2,2,128,128]{3,2,1,0:T(8,128)(2,1)S(1)}, bf16[2,2,128,128]{3,2,1,0:T(8,128)(2,1)S(1)}, u32[]{:S(2)}, u32[]{:S(2)}) collective-permute-start(bf16[2,2,128,128]{3,2,1,0:T(8,128)(2,1)S(1)} %fusion.1), channel_id=1, source_target_pairs={{0,16},{16,32},{32,48},{48,64},{64,80},{80,96},{96,112},{112,128},... | collective-permute-start | bytes 393224 | tf_op jit(solution)/shard_map/ppermute | solution.py:15
  51.9 16.4 %all-to-all-start.1 = ((bf16[16,64,128]{2,1,0:T(8,128)(2,1)}), bf16[16,64,128]{2,1,0:T(8,128)(2,1)S(1)}, u32[]{:S(2)}, u32[]{:S(2)}) async-start(bf16[16,64,128]{2,1,0:T(8,128)(2,1)} %broadcast_in_dim.2), calls=%async_computation.1 | async-start | bytes 524288 | tf_op jit(solution)/shard_map/all_to_all | solution.py:237

commit v4 on v3

--- a/solution.py
+++ b/solution.py
@@ -119,76 +119,82 @@
         both = jnp.concatenate([ext_ref[side, layer, part, rows, :] for side in range(2)], 1)
         return twice(pltpu.roll(both, lax.rem(2 * size - col, 2 * size), 1)[:, :size])
 
-    slots = range(measured_ref.shape[0])
-    corners = [(corner_ref[slot, 0], corner_ref[slot, 1]) for slot in slots]
-    patches = [
-        [[load_patch(row, col, layer, part) for part in range(2)] for layer in range(layers)]
-        for row, col in corners
-    ]
-    units = [(which, pair) for which in slots for pair in range(pairs)]
-    prop = [twice(prop_ref[part]) for part in range(2)]
-    probe = [
-        tuple(
-            jnp.concatenate([probe_ref[2 * pair, part], probe_ref[2 * pair + 1, part]], 1)
-            for part in range(2)
+    def visit(count):
+        slots = range(count)
+        corners = [(corner_ref[slot, 0], corner_ref[slot, 1]) for slot in slots]
+        patches = [
+            [[load_patch(row, col, layer, part) for part in range(2)] for layer in range(layers)]
+            for row, col in corners
+        ]
+        units = [(which, pair) for which in slots for pair in range(pairs)]
+        prop = [twice(prop_ref[part]) for part in range(2)]
+        probe = [
+            tuple(
+                jnp.concatenate([probe_ref[2 * pair, part], probe_ref[2 * pair + 1, part]], 1)
+                for part in range(2)
+            )
+            for pair in range(pairs)
+        ]
+        entering = [[probe[pair] for _, pair in units]]
+        for layer in range(layers):
+            leaving = [
+                multiply(*wave, *patches[which][layer])
+                for wave, (which, _) in zip(entering[layer], units)
+            ]
+            freqs = forward(leaving)
+            if layer < layers - 1:
+                entering.append(inverse([multiply(*freq, *prop) for freq in freqs]))
+        far = freqs
+        residuals = []
+        for which, slot in enumerate(slots):
+            power = sum(
+                real * real + imag * imag
+                for (real, imag), unit in zip(far, units)
+                if unit[0] == which
+            )
+            residual = jnp.where(slot < counts_ref[0], fold(power) - measured_ref[slot], 0.0)
+            residuals.append(twice(residual))
+        back = inverse(
+            [
+                (residuals[which] * real, residuals[which] * imag)
+                for (real, imag), (which, _) in zip(far, units)
+            ]
         )
-        for pair in range(pairs)
-    ]
-    entering = [[probe[pair] for _, pair in units]]
-    for layer in range(layers):
-        leaving = [
-            multiply(*wave, *patches[which][layer])
-            for wave, (which, _) in zip(entering[layer], units)
-        ]
-        freqs = forward(leaving)
-        if layer < layers - 1:
-            entering.append(inverse([multiply(*freq, *prop) for freq in freqs]))
-    far = freqs
-    residuals = []
-    for which, slot in enumerate(slots):
-        power = sum(
-            real * real + imag * imag
-            for (real, imag), unit in zip(far, units)
-            if unit[0] == which
-        )
-        residual = jnp.where(slot < counts_ref[0], fold(power) - measured_ref[slot], 0.0)
-        residuals.append(twice(residual))
-    back = inverse(
-        [
-            (residuals[which] * real, residuals[which] * imag)
-            for (real, imag), (which, _) in zip(far, units)
-        ]
-    )
-    for layer in reversed(range(layers)):
-        terms = [
-            multiply_conj(*wave, *entered) for wave, entered in zip(back, entering[layer])
-        ]
-        for which, (row, col) in enumerate(corners):
+        for layer in reversed(range(layers)):
+            terms = [
+                multiply_conj(*wave, *entered) for wave, entered in zip(back, entering[layer])
+            ]
+            for which, (row, col) in enumerate(corners):
+                for part in range(2):
+                    block = fold(
+                        sum(term[part] for term, unit in zip(terms, units) if unit[0] == which)
+                    )
+                    wide = jnp.concatenate([block, jnp.zeros_like(block)], 1)
+                    wide = pltpu.roll(wide, col, 1)
+                    rows = pl.ds(row, size)
+                    acc_ref[0, layer, part, rows, :] += wide[:, :size]
+                    acc_ref[1, layer, part, rows, :] += wide[:, size:]
+            to_enter = [
+                multiply_conj(*wave, *patches[which][layer])
+                for wave, (which, _) in zip(back, units)
+            ]
+            if layer > 0:
+                back = inverse([multiply_conj(*freq, *prop) for freq in forward(to_enter)])
+        for pair in range(pairs):
             for part in range(2):
-                block = fold(
-                    sum(term[part] for term, unit in zip(terms, units) if unit[0] == which)
-                )
-                wide = jnp.concatenate([block, jnp.zeros_like(block)], 1)
-                wide = pltpu.roll(wide, col, 1)
-                rows = pl.ds(row, size)
-                acc_ref[0, layer, part, rows, :] += wide[:, :size]
-                acc_ref[1, layer, part, rows, :] += wide[:, size:]
-        to_enter = [
-            multiply_conj(*wave, *patches[which][layer])
-            for wave, (which, _) in zip(back, units)
-        ]
-        if layer > 0:
-            back = inverse([multiply_conj(*freq, *prop) for freq in forward(to_enter)])
-    for pair in range(pairs):
-        for part in range(2):
-            both = sum(wave[part] for wave, unit in zip(to_enter, units) if unit[1] == pair)
-            both = both.astype(bf16)
-            probe_out_ref[2 * pair, part] = both[:, :size]
-            probe_out_ref[2 * pair + 1, part] = both[:, size:]
+                both = sum(wave[part] for wave, unit in zip(to_enter, units) if unit[1] == pair)
+                both = both.astype(bf16)
+                probe_out_ref[2 * pair, part] = both[:, :size]
+                probe_out_ref[2 * pair + 1, part] = both[:, size:]
+
+    most = measured_ref.shape[0]
+    few = (most + 1) // 2
+    pl.when(counts_ref[0] <= few)(lambda: visit(few))
+    pl.when(counts_ref[0] > few)(lambda: visit(most))
     grad_ref[...] = acc_ref[0, :, :, :size]
-    side_ref[0] = acc_ref[1, :, :, :size].astype(bf16)
-    side_ref[1] = acc_ref[1, :, :, size:].astype(bf16)
-    foot_ref[...] = acc_ref[0, :, :, size:]
+    side_ref[...] = acc_ref[1, :, :, :size]
+    foot_ref[0] = acc_ref[0, :, :, size:].astype(bf16)
+    foot_ref[1] = acc_ref[1, :, :, size:].astype(bf16)
 
 
 def local_grads(own, right, lower, probe_modes, prop, measured, dft, counts, corners):
@@ -201,8 +207,8 @@
         grads_kernel,
         out_shape=(
             jax.ShapeDtypeStruct(tile, f32),
+            jax.ShapeDtypeStruct(tile, f32),
             jax.ShapeDtypeStruct((2,) + tile, bf16),
-            jax.ShapeDtypeStruct(tile, f32),
             jax.ShapeDtypeStruct(probe_modes.shape, bf16),
         ),
         in_specs=[smem] * 2 + [vmem] * 7,
@@ -228,16 +234,15 @@
     grad, side, foot, probe_part = local_grads(
         object_slices, right, lower, probe_modes, prop, measured, dft, counts, corners
     )
-    side_back = from_behind(side, "col", 1).astype(jnp.float32)
+    foot_back = from_behind(foot, "row", 1).astype(jnp.float32)
     shares = probe_part.reshape(col_count, -1, probe_part.shape[-1])
     received = lax.all_to_all(shares, "col", 0, 0, tiled=True)
-    foot_back = from_behind((foot + side_back[1]).astype(jnp.bfloat16), "row", 1)
-    received, foot_back = lax.optimization_barrier((received, foot_back))
+    side_back = from_behind((side + foot_back[1]).astype(jnp.bfloat16), "col", 1)
     share = jnp.sum(received.astype(jnp.float32), 0).astype(jnp.bfloat16)
     spread = lax.all_to_all(
         jnp.broadcast_to(share[None], shares.shape), "col", 0, 0, tiled=True
     )
-    owned = grad + side_back[0] + foot_back.astype(jnp.float32)
+    owned = grad + foot_back[0] + side_back.astype(jnp.float32)
     region_slots = measured.shape[0] * col_count
     probe_total = spread.reshape(probe_part.shape).astype(jnp.float32)
     return (owned, (probe_total * (1.0 / math.sqrt(region_slots)))[None])

time: 69.9 us -> 68.3 us (0.977)
  waiting for transfers between devices: 29.8 us -> 26.6 us
  starting transfers between devices: 28 us -> 31 us
  Pallas kernels: 6.34 us -> 4.43 us
    all_to_all x1, waiting for transfers between devices: 11 us -> 3.57 us  [body(): lax.all_to_all(jnp.broadcast_to(share[None], shares.shape), 'col', 0, 0,...]
    ppermute x4, waiting for transfers between devices: 13.9 us -> 19.9 us  [from_behind(): return lax.ppermute(block, axis, route)]
    pallas_call x1, Pallas kernels: 6.34 us -> 4.43 us  [local_grads(): pl.pallas_call(grads_kernel, out_shape=(jax.ShapeDtypeStruct(tile, f32),...]
    all_to_all x1, waiting for transfers between devices: 4.82 us -> 3.05 us  [body(): received = lax.all_to_all(shares, 'col', 0, 0, tiled=True)]
    all_to_all x1, starting transfers between devices: 4.61 us -> 6.31 us  [body(): lax.all_to_all(jnp.broadcast_to(share[None], shares.shape), 'col', 0, 0,...]
    all_to_all x1, starting transfers between devices: 12.2 us -> 13.7 us  [body(): received = lax.all_to_all(shares, 'col', 0, 0, tiled=True)]
  transfers between devices with their start and end apart: 6 -> 6, of which waited for: 5 -> 6; matrix products, arithmetic and copies ran while one was open for 3% -> 3% of each run, Pallas kernels for 0% -> 0%
where the time goes in v4:
time: 68.3 us; the launch traced here: 67 us
  starting transfers between devices  31 us (45%)
  waiting for transfers between devices  26.6 us (39%)
  Pallas kernels  4.43 us (6%)
  other arithmetic  2.41 us (4%)
  between operations  1.44 us (2%)
  local copies, waits for them, and re-layouts  1.12 us (2%)
    ppermute x4, waiting for transfers between devices, from_behind(): return lax.ppermute(block, axis, route)  19.9 us
    all_to_all x1, starting transfers between devices, body(): received = lax.all_to_all(shares, 'col', 0, 0, tiled=True)  13.7 us
    ppermute x4, starting transfers between devices, from_behind(): return lax.ppermute(block, axis, route)  11 us
    all_to_all x1, starting transfers between devices, body(): lax.all_to_all(jnp.broadcast_to(share[None], shares.shape), 'col', 0, 0,...  6.31 us
    pallas_call x1, Pallas kernels, local_grads(): pl.pallas_call(grads_kernel, out_shape=(jax.ShapeDtypeStruct(tile, f32),...  4.43 us
    all_to_all x1, waiting for transfers between devices, body(): lax.all_to_all(jnp.broadcast_to(share[None], shares.shape), 'col', 0, 0,...  3.57 us
    all_to_all x1, waiting for transfers between devices, body(): received = lax.all_to_all(shares, 'col', 0, 0, tiled=True)  3.05 us
  transfers between devices with their start and end apart: 6, of which 6 were waited for; matrix products, arithmetic and copies ran while one was open for 3% of the time, Pallas kernels for 0%

profile of v4, /device:TPU:56, one launch (start us, length us, event | category | flops | bytes accessed | tf_op | source)
XLA Modules:
  0.0 67.0 jit_solution(5087088964066383011)
XLA Ops:
  0.6 0.0 copy-start.3
  0.6 1.4 %collective-permute-start = (bf16[2,2,128,128]{3,2,1,0:T(8,128)(2,1)}, bf16[2,2,128,128]{3,2,1,0:T(8,128)(2,1)S(1)}, u32[]{:S(2)}, u32[]{:S(2)}) collective-permute-start(bf16[2,2,128,128]{3,2,1,0:T(8,128)(2,1)} %own_ref.1), channel_id=1, source_target_pairs={{1,0},{2,1},{3,2},{4,3},{5,4},{6,5},{7,6},{8,7},{9,8},{10,9},{11,1... | collective-permute-start | bytes 393224 | tf_op jit(solution)/shard_map/ppermute | solution.py:15
  2.1 0.3 fusion.14
  2.3 0.3 multiply_convert_fusion
  2.6 0.0 copy-done.3
  2.6 0.2 cosine_bitcast_fusion
  2.9 0.0 copy-start.1
  2.9 0.0 copy-start
  3.0 5.8 %collective-permute-done.right_ref = bf16[2,2,128,128]{3,2,1,0:T(8,128)(2,1)S(1)} collective-permute-done((bf16[2,2,128,128]{3,2,1,0:T(8,128)(2,1)}, bf16[2,2,128,128]{3,2,1,0:T(8,128)(2,1)S(1)}, u32[]{:S(2)}, u32[]{:S(2)}) %collective-permute-start) | collective-permute-done | bytes 131104 | tf_op jit(solution)/shard_map/ppermute | solution.py:15
  8.8 0.0 copy-done.1
  8.8 0.0 copy-start.2
  8.8 3.2 %collective-permute-start.1 = (bf16[2,2,2,128,128]{4,3,2,1,0:T(8,128)(2,1)S(1)}, bf16[2,2,2,128,128]{4,3,2,1,0:T(8,128)(2,1)S(1)}, u32[]{:S(2)}, u32[]{:S(2)}) collective-permute-start(bf16[2,2,2,128,128]{4,3,2,1,0:T(8,128)(2,1)S(1)} %pad_maximum_fusion), channel_id=1, source_target_pairs={{16,0},{32,16},{48,32},{64,48},{80,64},{96,80},{112,96},{128,112},... | collective-permute-start | bytes 786440 | tf_op jit(solution)/shard_map/ppermute | solution.py:15
  12.0 0.1 pad_add_fusion
  12.1 0.0 copy-start.4
  12.7 0.0 copy-done.4
  12.8 0.1 copy.8
  12.9 3.0 %collective-permute-done.1.lower_ref = bf16[2,2,2,128,128]{4,3,2,1,0:T(8,128)(2,1)S(1)} collective-permute-done((bf16[2,2,2,128,128]{4,3,2,1,0:T(8,128)(2,1)S(1)}, bf16[2,2,2,128,128]{4,3,2,1,0:T(8,128)(2,1)S(1)}, u32[]{:S(2)}, u32[]{:S(2)}) %collective-permute-start.1) | collective-permute-done | bytes 262176 | tf_op jit(solution)/shard_map/ppermute | solution.py:15
  15.9 0.0 copy-done
  15.9 0.0 copy-done.2
  15.9 4.4 %shard_map.77 = (f32[2,2,128,128]{3,2,1,0:T(8,128)S(1)}, f32[2,2,128,128]{3,2,1,0:T(8,128)S(1)}, bf16[2,2,2,128,128]{4,3,2,1,0:T(8,128)(2,1)S(1)}, bf16[4,2,128,128]{3,2,1,0:T(8,128)(2,1)}) custom-call(s32[1]{0:T(128)S(6)} %copy.9.counts_ref, s32[4,2]{1,0:T(4,128)S(1)} %broadcast_subtract_fusion.corner_ref, bf16[2,2,128,128]{3,2,1,0:T(8,128)(2,1)S(1)} %copy-done.1, ...), custom_call_target="tpu_custom_call" | custom-call | tf_op jit(solution)/shard_map/pallas_call | solution.py:206
  20.3 13.7 %all-to-all-start = ((bf16[16,64,128]{2,1,0:T(8,128)(2,1)}), bf16[16,64,128]{2,1,0:T(8,128)(2,1)S(1)}, u32[]{:S(2)}, u32[]{:S(2)}) async-start(bf16[16,64,128]{2,1,0:T(8,128)(2,1)} %bitcast.10), calls=%async_computation | async-start | bytes 524288 | tf_op jit(solution)/shard_map/all_to_all | solution.py:239
  34.0 2.6 %collective-permute-start.2 = (bf16[2,2,2,128,128]{4,3,2,1,0:T(8,128)(2,1)S(1)}, bf16[2,2,2,128,128]{4,3,2,1,0:T(8,128)(2,1)S(1)}, u32[]{:S(2)}, u32[]{:S(2)}) collective-permute-start(bf16[2,2,2,128,128]{4,3,2,1,0:T(8,128)(2,1)S(1)} %get-tuple-element.7), channel_id=1, source_target_pairs={{0,16},{16,32},{32,48},{48,64},{64,80},{80,96},{96,112},{112,128},... | collective-permute-start | bytes 786440 | tf_op jit(solution)/shard_map/ppermute | solution.py:15
  36.5 7.0 %collective-permute-done.2 = bf16[2,2,2,128,128]{4,3,2,1,0:T(8,128)(2,1)S(1)} collective-permute-done((bf16[2,2,2,128,128]{4,3,2,1,0:T(8,128)(2,1)S(1)}, bf16[2,2,2,128,128]{4,3,2,1,0:T(8,128)(2,1)S(1)}, u32[]{:S(2)}, u32[]{:S(2)}) %collective-permute-start.2) | collective-permute-done | bytes 262176 | tf_op jit(solution)/shard_map/ppermute | solution.py:15
  43.6 3.1 %all-to-all-done = bf16[16,64,128]{2,1,0:T(8,128)(2,1)S(1)} async-done(((bf16[16,64,128]{2,1,0:T(8,128)(2,1)}), bf16[16,64,128]{2,1,0:T(8,128)(2,1)S(1)}, u32[]{:S(2)}, u32[]{:S(2)}) %all-to-all-start) | async-done | bytes 262176 | tf_op jit(solution)/shard_map/all_to_all | solution.py:239
  46.7 0.8 %broadcast_in_dim.2 = bf16[16,64,128]{2,1,0:T(8,128)(2,1)} broadcast(bf16[64,128]{1,0:T(8,128)(2,1)S(1)} %reduce_sum.12), dimensions={1,2} | broadcast | bytes 278528 | tf_op jit(solution)/shard_map/broadcast_in_dim | solution.py:243
  47.4 6.3 %all-to-all-start.1 = ((bf16[16,64,128]{2,1,0:T(8,128)(2,1)}), bf16[16,64,128]{2,1,0:T(8,128)(2,1)S(1)}, u32[]{:S(2)}, u32[]{:S(2)}) async-start(bf16[16,64,128]{2,1,0:T(8,128)(2,1)} %broadcast_in_dim.2), calls=%async_computation.1 | async-start | bytes 524288 | tf_op jit(solution)/shard_map/all_to_all | solution.py:242
  53.8 3.8 %collective-permute-start.3 = (bf16[2,2,128,128]{3,2,1,0:T(8,128)(2,1)S(1)}, bf16[2,2,128,128]{3,2,1,0:T(8,128)(2,1)S(1)}, u32[]{:S(2)}, u32[]{:S(2)}) collective-permute-start(bf16[2,2,128,128]{3,2,1,0:T(8,128)(2,1)S(1)} %fusion.1), channel_id=1, source_target_pairs={{0,1},{1,2},{2,3},{3,4},{4,5},{5,6},{6,7},{7,8},{8,9},{9,10},{10,1... | collective-permute-start | bytes 393224 | tf_op jit(solution)/shard_map/ppermute | solution.py:15
  57.6 4.2 %collective-permute-done.3 = bf16[2,2,128,128]{3,2,1,0:T(8,128)(2,1)S(1)} collective-permute-done((bf16[2,2,128,128]{3,2,1,0:T(8,128)(2,1)S(1)}, bf16[2,2,128,128]{3,2,1,0:T(8,128)(2,1)S(1)}, u32[]{:S(2)}, u32[]{:S(2)}) %collective-permute-start.3) | collective-permute-done | bytes 131104 | tf_op jit(solution)/shard_map/ppermute | solution.py:15
  61.8 0.7 %fusion.3 = f32[2,2,128,128]{3,2,1,0:T(8,128)} fusion(f32[2,2,128,128]{3,2,1,0:T(8,128)S(1)} %get-tuple-element.6, f32[2,2,2,128,128]{4,3,2,1,0:T(8,128)S(1)} %convert_element_type.60, bf16[2,2,128,128]{3,2,1,0:T(8,128)(2,1)S(1)} %collective-permute-done.3), kind=kLoop, calls=%fused_computation.6 | loop fusion | flops 196608 | bytes 917504 | tf_op jit(solution)/shard_map/add | solution.py:245
  62.5 3.6 %all-to-all-done.1 = bf16[16,64,128]{2,1,0:T(8,128)(2,1)S(1)} async-done(((bf16[16,64,128]{2,1,0:T(8,128)(2,1)}), bf16[16,64,128]{2,1,0:T(8,128)(2,1)S(1)}, u32[]{:S(2)}, u32[]{:S(2)}) %all-to-all-start.1) | async-done | bytes 262176 | tf_op jit(solution)/shard_map/all_to_all | solution.py:242
  66.1 0.8 %convert_multiply_fusion = f32[16,64,128]{2,1,0:T(8,128)} fusion(bf16[16,64,128]{2,1,0:T(8,128)(2,1)S(1)} %all-to-all-done.1), kind=kLoop, calls=%fused_computation | loop fusion | flops 262144 | bytes 786432 | tf_op jit(solution)/shard_map/mul | solution.py:248
  (8 shorter events, 0.2 us)
Async XLA Ops:
  0.6 2.0 %copy-start.3 = (f32[128,128]{1,0:T(8,128)S(1)}, f32[128,128]{1,0:T(8,128)}, u32[]{:S(2)}) copy-start(f32[128,128]{1,0:T(8,128)} %param.8) | copy-start | bytes 196612
  0.6 8.1 %collective-permute-start = (bf16[2,2,128,128]{3,2,1,0:T(8,128)(2,1)}, bf16[2,2,128,128]{3,2,1,0:T(8,128)(2,1)S(1)}, u32[]{:S(2)}, u32[]{:S(2)}) collective-permute-start(bf16[2,2,128,128]{3,2,1,0:T(8,128)(2,1)} %own_ref.1), channel_id=1, source_target_pairs={{1,0},{2,1},{3,2},{4,3},{5,4},{6,5},{7,6},{8,7},{9,8},{10,9},{11,1... | collective-permute-start | bytes 393224 | tf_op jit(solution)/shard_map/ppermute | solution.py:15
  2.9 5.8 %copy-start.1 = (bf16[2,2,128,128]{3,2,1,0:T(8,128)(2,1)S(1)}, bf16[2,2,128,128]{3,2,1,0:T(8,128)(2,1)}, u32[]{:S(2)}) copy-start(bf16[2,2,128,128]{3,2,1,0:T(8,128)(2,1)} %own_ref.1) | copy-start | bytes 393220
  2.9 12.9 %copy-start = (f32[4,2,128,128]{3,2,1,0:T(8,128)S(1)}, f32[4,2,128,128]{3,2,1,0:T(8,128)}, u32[]{:S(2)}) copy-start(f32[4,2,128,128]{3,2,1,0:T(8,128)} %probe_ref.1) | copy-start | bytes 1572868
  8.8 7.1 %copy-start.2 = (f32[4,128,128]{2,1,0:T(8,128)S(1)}, f32[4,128,128]{2,1,0:T(8,128)}, u32[]{:S(2)}) copy-start(f32[4,128,128]{2,1,0:T(8,128)} %measured_ref.1) | copy-start | bytes 786436
  8.8 7.1 %collective-permute-start.1 = (bf16[2,2,2,128,128]{4,3,2,1,0:T(8,128)(2,1)S(1)}, bf16[2,2,2,128,128]{4,3,2,1,0:T(8,128)(2,1)S(1)}, u32[]{:S(2)}, u32[]{:S(2)}) collective-permute-start(bf16[2,2,2,128,128]{4,3,2,1,0:T(8,128)(2,1)S(1)} %pad_maximum_fusion), channel_id=1, source_target_pairs={{16,0},{32,16},{48,32},{64,48},{80,64},{96,80},{112,96},{128,112},... | collective-permute-start | bytes 786440 | tf_op jit(solution)/shard_map/ppermute | solution.py:15
  12.1 0.7 %copy-start.4 = (s32[4,2]{0,1:T(2,128)S(1)}, s32[4,2]{0,1:T(2,128)}, u32[]{:S(2)}) copy-start(s32[4,2]{0,1:T(2,128)} %param.11) | copy-start | bytes 100
  20.3 26.3 %all-to-all-start = ((bf16[16,64,128]{2,1,0:T(8,128)(2,1)}), bf16[16,64,128]{2,1,0:T(8,128)(2,1)S(1)}, u32[]{:S(2)}, u32[]{:S(2)}) async-start(bf16[16,64,128]{2,1,0:T(8,128)(2,1)} %bitcast.10), calls=%async_computation | async-start | bytes 524288 | tf_op jit(solution)/shard_map/all_to_all | solution.py:239
  34.0 9.6 %collective-permute-start.2 = (bf16[2,2,2,128,128]{4,3,2,1,0:T(8,128)(2,1)S(1)}, bf16[2,2,2,128,128]{4,3,2,1,0:T(8,128)(2,1)S(1)}, u32[]{:S(2)}, u32[]{:S(2)}) collective-permute-start(bf16[2,2,2,128,128]{4,3,2,1,0:T(8,128)(2,1)S(1)} %get-tuple-element.7), channel_id=1, source_target_pairs={{0,16},{16,32},{32,48},{48,64},{64,80},{80,96},{96,112},{112,128},... | collective-permute-start | bytes 786440 | tf_op jit(solution)/shard_map/ppermute | solution.py:15
  47.4 18.7 %all-to-all-start.1 = ((bf16[16,64,128]{2,1,0:T(8,128)(2,1)}), bf16[16,64,128]{2,1,0:T(8,128)(2,1)S(1)}, u32[]{:S(2)}, u32[]{:S(2)}) async-start(bf16[16,64,128]{2,1,0:T(8,128)(2,1)} %broadcast_in_dim.2), calls=%async_computation.1 | async-start | bytes 524288 | tf_op jit(solution)/shard_map/all_to_all | solution.py:242
  53.8 8.0 %collective-permute-start.3 = (bf16[2,2,128,128]{3,2,1,0:T(8,128)(2,1)S(1)}, bf16[2,2,128,128]{3,2,1,0:T(8,128)(2,1)S(1)}, u32[]{:S(2)}, u32[]{:S(2)}) collective-permute-start(bf16[2,2,128,128]{3,2,1,0:T(8,128)(2,1)S(1)} %fusion.1), channel_id=1, source_target_pairs={{0,1},{1,2},{2,3},{3,4},{4,5},{5,6},{6,7},{7,8},{8,9},{9,10},{10,1... | collective-permute-start | bytes 393224 | tf_op jit(solution)/shard_map/ppermute | solution.py:15

commit v5 on v4

--- a/solution.py
+++ b/solution.py
@@ -221,6 +221,26 @@
     )(counts, corners, own, right, lower, probe_modes, prop, measured, dft)
 
 
+def finish_kernel(grad_ref, foot_ref, side_ref, spread_ref, owned_ref, probe_ref, *, scale):
+    f32 = jnp.float32
+    owned_ref[...] = grad_ref[...] + foot_ref[0].astype(f32) + side_ref[...].astype(f32)
+    probe_ref[...] = spread_ref[...].astype(f32) * scale
+
+
+def finish(grad, foot_back, side_back, spread, scale):
+    vmem = pl.BlockSpec(memory_space=pltpu.VMEM)
+    return pl.pallas_call(
+        functools.partial(finish_kernel, scale=scale),
+        out_shape=(
+            jax.ShapeDtypeStruct(grad.shape, jnp.float32),
+            jax.ShapeDtypeStruct(spread.shape, jnp.float32),
+        ),
+        in_specs=[vmem] * 4,
+        out_specs=(vmem,) * 2,
+        compiler_params=pltpu.CompilerParams(vmem_limit_bytes=16 * 1024 * 1024),
+    )(grad, foot_back, side_back, spread)
+
+
 def body(object_slices, probe_modes, prop_phase, measured, counts, coords):
     tile_rows = object_slices.shape[2]
     tile_cols = object_slices.shape[3]
@@ -234,18 +254,19 @@
     grad, side, foot, probe_part = local_grads(
         object_slices, right, lower, probe_modes, prop, measured, dft, counts, corners
     )
-    foot_back = from_behind(foot, "row", 1).astype(jnp.float32)
+    foot_back = from_behind(foot, "row", 1)
     shares = probe_part.reshape(col_count, -1, probe_part.shape[-1])
     received = lax.all_to_all(shares, "col", 0, 0, tiled=True)
-    side_back = from_behind((side + foot_back[1]).astype(jnp.bfloat16), "col", 1)
+    side_back = from_behind((side + foot_back[1].astype(jnp.float32)).astype(jnp.bfloat16), "col", 1)
     share = jnp.sum(received.astype(jnp.float32), 0).astype(jnp.bfloat16)
     spread = lax.all_to_all(
         jnp.broadcast_to(share[None], shares.shape), "col", 0, 0, tiled=True
     )
-    owned = grad + foot_back[0] + side_back.astype(jnp.float32)
     region_slots = measured.shape[0] * col_count
-    probe_total = spread.reshape(probe_part.shape).astype(jnp.float32)
-    return (owned, (probe_total * (1.0 / math.sqrt(region_slots)))[None])
+    owned, probe_total = finish(
+        grad, foot_back, side_back, spread, 1.0 / math.sqrt(region_slots)
+    )
+    return (owned, probe_total.reshape((1,) + probe_part.shape))
 
 
 def solution(mesh):

time: 68.3 us -> 66.3 us (0.971); the launches traced: 67 us -> 65.8 us
  starting transfers between devices: 31 us -> 27.2 us
  Pallas kernels: 4.43 us -> 7.35 us
  other arithmetic: 2.41 us -> 0.79 us
  waiting for transfers between devices: 26.6 us -> 27.9 us
    all_to_all x1, waiting for transfers between devices: 3.05 us -> 10 us  [body(): received = lax.all_to_all(shares, 'col', 0, 0, tiled=True)]
    ppermute x4, waiting for transfers between devices: 19.9 us -> 13.4 us  [from_behind(): return lax.ppermute(block, axis, route)]
    all_to_all x1, starting transfers between devices: 13.7 us -> 11.6 us  [body(): received = lax.all_to_all(shares, 'col', 0, 0, tiled=True)]
    pallas_call x1, Pallas kernels: 4.43 us -> 6.44 us  [local_grads(): pl.pallas_call(grads_kernel, out_shape=(jax.ShapeDtypeStruct(tile, f32),...]
    all_to_all x1, starting transfers between devices: 6.31 us -> 4.61 us  [body(): lax.all_to_all(jnp.broadcast_to(share[None], shares.shape), 'col', 0, 0,...]
    all_to_all x1, waiting for transfers between devices: 3.57 us -> 4.5 us  [body(): lax.all_to_all(jnp.broadcast_to(share[None], shares.shape), 'col', 0, 0,...]
    pallas_call x0 -> x1, Pallas kernels: none -> 0.92 us  [finish(): pl.pallas_call(functools.partial(finish_kernel, scale=scale), out_shape=(...]
    mul x1 -> x0, other arithmetic: 0.85 us -> none  [body(): return (owned, (probe_total * (1.0 / math.sqrt(region_slots)))[None])]
  transfers between devices with their start and end apart: 6 -> 6, of which waited for: 6 -> 5; matrix products, arithmetic and copies ran while one was open for 3% -> 3% of each run, Pallas kernels for 0% -> 0%
where the time goes in v5:
time: 66.3 us; the launch traced here: 65.8 us
  waiting for transfers between devices  27.9 us (42%)
  starting transfers between devices  27.2 us (41%)
  Pallas kernels  7.35 us (11%)
  between operations  1.45 us (2%)
  local copies, waits for them, and re-layouts  1.12 us (2%)
  other arithmetic  0.79 us (1%)
    ppermute x4, waiting for transfers between devices, from_behind(): return lax.ppermute(block, axis, route)  13.4 us
    all_to_all x1, starting transfers between devices, body(): received = lax.all_to_all(shares, 'col', 0, 0, tiled=True)  11.6 us
    ppermute x4, starting transfers between devices, from_behind(): return lax.ppermute(block, axis, route)  11 us
    all_to_all x1, waiting for transfers between devices, body(): received = lax.all_to_all(shares, 'col', 0, 0, tiled=True)  10 us
    pallas_call x1, Pallas kernels, local_grads(): pl.pallas_call(grads_kernel, out_shape=(jax.ShapeDtypeStruct(tile, f32),...  6.44 us
    all_to_all x1, starting transfers between devices, body(): lax.all_to_all(jnp.broadcast_to(share[None], shares.shape), 'col', 0, 0,...  4.61 us
    all_to_all x1, waiting for transfers between devices, body(): lax.all_to_all(jnp.broadcast_to(share[None], shares.shape), 'col', 0, 0,...  4.5 us
  transfers between devices with their start and end apart: 6, of which 5 were waited for; matrix products, arithmetic and copies ran while one was open for 3% of the time, Pallas kernels for 0%

profile of v5, /device:TPU:56, one launch (start us, length us, event | category | flops | bytes accessed | tf_op | source)
XLA Modules:
  0.0 65.8 jit_solution(13522000575575232080)
XLA Ops:
  0.6 0.0 copy-start.3
  0.6 1.4 %collective-permute-start = (bf16[2,2,128,128]{3,2,1,0:T(8,128)(2,1)}, bf16[2,2,128,128]{3,2,1,0:T(8,128)(2,1)S(1)}, u32[]{:S(2)}, u32[]{:S(2)}) collective-permute-start(bf16[2,2,128,128]{3,2,1,0:T(8,128)(2,1)} %own_ref.1), channel_id=1, source_target_pairs={{1,0},{2,1},{3,2},{4,3},{5,4},{6,5},{7,6},{8,7},{9,8},{10,9},{11,1... | collective-permute-start | bytes 393224 | tf_op jit(solution)/shard_map/ppermute | solution.py:15
  2.1 0.3 fusion.11
  2.3 0.3 multiply_convert_fusion
  2.6 0.0 copy-done.3
  2.6 0.2 cosine_bitcast_fusion
  2.9 0.0 copy-start.1
  2.9 0.0 copy-start
  3.0 5.8 %collective-permute-done.right_ref = bf16[2,2,128,128]{3,2,1,0:T(8,128)(2,1)S(1)} collective-permute-done((bf16[2,2,128,128]{3,2,1,0:T(8,128)(2,1)}, bf16[2,2,128,128]{3,2,1,0:T(8,128)(2,1)S(1)}, u32[]{:S(2)}, u32[]{:S(2)}) %collective-permute-start) | collective-permute-done | bytes 131104 | tf_op jit(solution)/shard_map/ppermute | solution.py:15
  8.8 0.0 copy-done.1
  8.8 0.0 copy-start.2
  8.8 3.2 %collective-permute-start.1 = (bf16[2,2,2,128,128]{4,3,2,1,0:T(8,128)(2,1)S(1)}, bf16[2,2,2,128,128]{4,3,2,1,0:T(8,128)(2,1)S(1)}, u32[]{:S(2)}, u32[]{:S(2)}) collective-permute-start(bf16[2,2,2,128,128]{4,3,2,1,0:T(8,128)(2,1)S(1)} %pad_maximum_fusion), channel_id=1, source_target_pairs={{16,0},{32,16},{48,32},{64,48},{80,64},{96,80},{112,96},{128,112},... | collective-permute-start | bytes 786440 | tf_op jit(solution)/shard_map/ppermute | solution.py:15
  12.0 0.1 pad_add_fusion
  12.1 0.0 copy-start.4
  12.7 0.0 copy-done.4
  12.8 0.1 copy.8
  12.9 3.0 %collective-permute-done.1.lower_ref = bf16[2,2,2,128,128]{4,3,2,1,0:T(8,128)(2,1)S(1)} collective-permute-done((bf16[2,2,2,128,128]{4,3,2,1,0:T(8,128)(2,1)S(1)}, bf16[2,2,2,128,128]{4,3,2,1,0:T(8,128)(2,1)S(1)}, u32[]{:S(2)}, u32[]{:S(2)}) %collective-permute-start.1) | collective-permute-done | bytes 262176 | tf_op jit(solution)/shard_map/ppermute | solution.py:15
  15.9 0.0 copy-done
  15.9 0.0 copy-done.2
  15.9 6.4 %shard_map.77 = (f32[2,2,128,128]{3,2,1,0:T(8,128)S(1)}, f32[2,2,128,128]{3,2,1,0:T(8,128)S(1)}, bf16[2,2,2,128,128]{4,3,2,1,0:T(8,128)(2,1)S(1)}, bf16[4,2,128,128]{3,2,1,0:T(8,128)(2,1)}) custom-call(s32[1]{0:T(128)S(6)} %copy.9.counts_ref, s32[4,2]{1,0:T(4,128)S(1)} %broadcast_subtract_fusion.corner_ref, bf16[2,2,128,128]{3,2,1,0:T(8,128)(2,1)S(1)} %copy-done.1, ...), custom_call_target="tpu_custom_call" | custom-call | tf_op jit(solution)/shard_map/pallas_call | solution.py:206
  22.3 11.6 %all-to-all-start = ((bf16[16,64,128]{2,1,0:T(8,128)(2,1)}), bf16[16,64,128]{2,1,0:T(8,128)(2,1)S(1)}, u32[]{:S(2)}, u32[]{:S(2)}) async-start(bf16[16,64,128]{2,1,0:T(8,128)(2,1)} %bitcast.9), calls=%async_computation | async-start | bytes 524288 | tf_op jit(solution)/shard_map/all_to_all | solution.py:259
  33.9 2.5 %collective-permute-start.2 = (bf16[2,2,2,128,128]{4,3,2,1,0:T(8,128)(2,1)S(1)}, bf16[2,2,2,128,128]{4,3,2,1,0:T(8,128)(2,1)S(1)}, u32[]{:S(2)}, u32[]{:S(2)}) collective-permute-start(bf16[2,2,2,128,128]{4,3,2,1,0:T(8,128)(2,1)S(1)} %get-tuple-element.9), channel_id=1, source_target_pairs={{0,16},{16,32},{32,48},{48,64},{64,80},{80,96},{96,112},{112,128},... | collective-permute-start | bytes 786440 | tf_op jit(solution)/shard_map/ppermute | solution.py:15
  36.4 10.0 %all-to-all-done = bf16[16,64,128]{2,1,0:T(8,128)(2,1)S(1)} async-done(((bf16[16,64,128]{2,1,0:T(8,128)(2,1)}), bf16[16,64,128]{2,1,0:T(8,128)(2,1)S(1)}, u32[]{:S(2)}, u32[]{:S(2)}) %all-to-all-start) | async-done | bytes 262176 | tf_op jit(solution)/shard_map/all_to_all | solution.py:259
  46.5 0.8 %broadcast_in_dim.2 = bf16[16,64,128]{2,1,0:T(8,128)(2,1)} broadcast(bf16[64,128]{1,0:T(8,128)(2,1)S(1)} %reduce_sum.12), dimensions={1,2} | broadcast | bytes 278528 | tf_op jit(solution)/shard_map/broadcast_in_dim | solution.py:263
  47.3 4.6 %all-to-all-start.1 = ((bf16[16,64,128]{2,1,0:T(8,128)(2,1)}), bf16[16,64,128]{2,1,0:T(8,128)(2,1)S(1)}, u32[]{:S(2)}, u32[]{:S(2)}) async-start(bf16[16,64,128]{2,1,0:T(8,128)(2,1)} %broadcast_in_dim.2), calls=%async_computation.1 | async-start | bytes 524288 | tf_op jit(solution)/shard_map/all_to_all | solution.py:262
  51.9 0.0 collective-permute-done.2.foot_ref
  52.0 3.8 %collective-permute-start.3 = (bf16[2,2,128,128]{3,2,1,0:T(8,128)(2,1)S(1)}, bf16[2,2,128,128]{3,2,1,0:T(8,128)(2,1)S(1)}, u32[]{:S(2)}, u32[]{:S(2)}) collective-permute-start(bf16[2,2,128,128]{3,2,1,0:T(8,128)(2,1)S(1)} %fusion), channel_id=1, source_target_pairs={{0,1},{1,2},{2,3},{3,4},{4,5},{5,6},{6,7},{7,8},{8,9},{9,10},{10,1... | collective-permute-start | bytes 393224 | tf_op jit(solution)/shard_map/ppermute | solution.py:15
  55.8 4.6 %collective-permute-done.3.side_ref = bf16[2,2,128,128]{3,2,1,0:T(8,128)(2,1)S(1)} collective-permute-done((bf16[2,2,128,128]{3,2,1,0:T(8,128)(2,1)S(1)}, bf16[2,2,128,128]{3,2,1,0:T(8,128)(2,1)S(1)}, u32[]{:S(2)}, u32[]{:S(2)}) %collective-permute-start.3) | collective-permute-done | bytes 131104 | tf_op jit(solution)/shard_map/ppermute | solution.py:15
  60.4 4.5 %all-to-all-done.1.spread_ref = bf16[16,64,128]{2,1,0:T(8,128)(2,1)S(1)} async-done(((bf16[16,64,128]{2,1,0:T(8,128)(2,1)}), bf16[16,64,128]{2,1,0:T(8,128)(2,1)S(1)}, u32[]{:S(2)}, u32[]{:S(2)}) %all-to-all-start.1) | async-done | bytes 262176 | tf_op jit(solution)/shard_map/all_to_all | solution.py:262
  64.9 0.9 %shard_map.78 = (f32[2,2,128,128]{3,2,1,0:T(8,128)}, f32[16,64,128]{2,1,0:T(8,128)}) custom-call(f32[2,2,128,128]{3,2,1,0:T(8,128)S(1)} %get-tuple-element.8.grad_ref, bf16[2,2,2,128,128]{4,3,2,1,0:T(8,128)(2,1)S(1)} %collective-permute-done.2.foot_ref, bf16[2,2,128,128]{3,2,1,0:T(8,128)(2,1)S(1)} %collective-permute-done.3.side_ref, ...), custom_call_target="tpu_custom_call" | custom-call | tf_op jit(solution)/shard_map/pallas_call | solution.py:232
  (7 shorter events, 0.2 us)
Async XLA Ops:
  0.6 2.0 %copy-start.3 = (f32[128,128]{1,0:T(8,128)S(1)}, f32[128,128]{1,0:T(8,128)}, u32[]{:S(2)}) copy-start(f32[128,128]{1,0:T(8,128)} %param.8) | copy-start | bytes 196612
  0.6 8.1 %collective-permute-start = (bf16[2,2,128,128]{3,2,1,0:T(8,128)(2,1)}, bf16[2,2,128,128]{3,2,1,0:T(8,128)(2,1)S(1)}, u32[]{:S(2)}, u32[]{:S(2)}) collective-permute-start(bf16[2,2,128,128]{3,2,1,0:T(8,128)(2,1)} %own_ref.1), channel_id=1, source_target_pairs={{1,0},{2,1},{3,2},{4,3},{5,4},{6,5},{7,6},{8,7},{9,8},{10,9},{11,1... | collective-permute-start | bytes 393224 | tf_op jit(solution)/shard_map/ppermute | solution.py:15
  2.9 5.8 %copy-start.1 = (bf16[2,2,128,128]{3,2,1,0:T(8,128)(2,1)S(1)}, bf16[2,2,128,128]{3,2,1,0:T(8,128)(2,1)}, u32[]{:S(2)}) copy-start(bf16[2,2,128,128]{3,2,1,0:T(8,128)(2,1)} %own_ref.1) | copy-start | bytes 393220
  2.9 12.9 %copy-start = (f32[4,2,128,128]{3,2,1,0:T(8,128)S(1)}, f32[4,2,128,128]{3,2,1,0:T(8,128)}, u32[]{:S(2)}) copy-start(f32[4,2,128,128]{3,2,1,0:T(8,128)} %probe_ref.1) | copy-start | bytes 1572868
  8.8 7.1 %copy-start.2 = (f32[4,128,128]{2,1,0:T(8,128)S(1)}, f32[4,128,128]{2,1,0:T(8,128)}, u32[]{:S(2)}) copy-start(f32[4,128,128]{2,1,0:T(8,128)} %measured_ref.1) | copy-start | bytes 786436
  8.8 7.1 %collective-permute-start.1 = (bf16[2,2,2,128,128]{4,3,2,1,0:T(8,128)(2,1)S(1)}, bf16[2,2,2,128,128]{4,3,2,1,0:T(8,128)(2,1)S(1)}, u32[]{:S(2)}, u32[]{:S(2)}) collective-permute-start(bf16[2,2,2,128,128]{4,3,2,1,0:T(8,128)(2,1)S(1)} %pad_maximum_fusion), channel_id=1, source_target_pairs={{16,0},{32,16},{48,32},{64,48},{80,64},{96,80},{112,96},{128,112},... | collective-permute-start | bytes 786440 | tf_op jit(solution)/shard_map/ppermute | solution.py:15
  12.1 0.7 %copy-start.4 = (s32[4,2]{0,1:T(2,128)S(1)}, s32[4,2]{0,1:T(2,128)}, u32[]{:S(2)}) copy-start(s32[4,2]{0,1:T(2,128)} %param.11) | copy-start | bytes 100
  22.3 24.2 %all-to-all-start = ((bf16[16,64,128]{2,1,0:T(8,128)(2,1)}), bf16[16,64,128]{2,1,0:T(8,128)(2,1)S(1)}, u32[]{:S(2)}, u32[]{:S(2)}) async-start(bf16[16,64,128]{2,1,0:T(8,128)(2,1)} %bitcast.9), calls=%async_computation | async-start | bytes 524288 | tf_op jit(solution)/shard_map/all_to_all | solution.py:259
  33.9 18.0 %collective-permute-start.2 = (bf16[2,2,2,128,128]{4,3,2,1,0:T(8,128)(2,1)S(1)}, bf16[2,2,2,128,128]{4,3,2,1,0:T(8,128)(2,1)S(1)}, u32[]{:S(2)}, u32[]{:S(2)}) collective-permute-start(bf16[2,2,2,128,128]{4,3,2,1,0:T(8,128)(2,1)S(1)} %get-tuple-element.9), channel_id=1, source_target_pairs={{0,16},{16,32},{32,48},{48,64},{64,80},{80,96},{96,112},{112,128},... | collective-permute-start | bytes 786440 | tf_op jit(solution)/shard_map/ppermute | solution.py:15
  47.3 17.6 %all-to-all-start.1 = ((bf16[16,64,128]{2,1,0:T(8,128)(2,1)}), bf16[16,64,128]{2,1,0:T(8,128)(2,1)S(1)}, u32[]{:S(2)}, u32[]{:S(2)}) async-start(bf16[16,64,128]{2,1,0:T(8,128)(2,1)} %broadcast_in_dim.2), calls=%async_computation.1 | async-start | bytes 524288 | tf_op jit(solution)/shard_map/all_to_all | solution.py:262
  52.0 8.5 %collective-permute-start.3 = (bf16[2,2,128,128]{3,2,1,0:T(8,128)(2,1)S(1)}, bf16[2,2,128,128]{3,2,1,0:T(8,128)(2,1)S(1)}, u32[]{:S(2)}, u32[]{:S(2)}) collective-permute-start(bf16[2,2,128,128]{3,2,1,0:T(8,128)(2,1)S(1)} %fusion), channel_id=1, source_target_pairs={{0,1},{1,2},{2,3},{3,4},{4,5},{5,6},{6,7},{7,8},{8,9},{9,10},{10,1... | collective-permute-start | bytes 393224 | tf_op jit(solution)/shard_map/ppermute | solution.py:15
